TPU v7x, 256 devices: a whole 4x4x8 slice. The times are simulated.
256 devices in a mesh: dp: 16 (over x_hi, y, core), seq: 16 (over z, x_lo).
Axes of the slice: x: 4 (x_hi: 2, x_lo: 2; x = x_hi * 2 + x_lo), y: 4, z: 8, core: 2. Of those that a mesh axis runs over, the one named last changes fastest.
Arguments:
- hidden_states: bfloat16 [16, 4096, 4096], P('dp', 'seq'), may hold values from -24 to 24
- query_weight: bfloat16 [4096, 2048], P('dp'), may hold values from -0.5 to 0.5
- key_matrix: bfloat16 [4096, 512], P('dp'), may hold values from -0.5 to 0.5
- value_matrix: bfloat16 [4096, 512], P('dp'), may hold values from -0.09375 to 0.09375
- context_lengths: int32 [16], P('dp'), may hold values from 128 to 4096, as said below
Outputs:
- attended: bfloat16 [16, 4096, 2048], P('dp', 'seq')
Inputs may be any that keep to these rules, and one draw needn't show every extreme that they name: `context_lengths`: every length is a multiple of 128, and some context has length 4096.
All inputs are finite; a program needn't handle non-finite values.
Results may differ from a plain program's by a relative error of at most 0.0072.
Values may be sent and summed in bfloat16 or wider, within the bound.
A program may use at most 128 MiB of HBM per device.

v0:
```python
import jax
import jax.numpy as jnp
from jax import lax
from jax.sharding import PartitionSpec as P

QUERY_HEADS = 16
KEY_VALUE_HEADS = 4
HEAD_WIDTH = 128
WINDOW_TOKENS = 2048


rope_base = 10000.0
negative_bound = -1e30


def from_behind(block, axis, distance):
    devices = range(lax.axis_size(axis))
    route = [(i - distance, i) for i in devices if i - distance in devices]
    return lax.ppermute(block, axis, route)


def apply_rotary(values_in, positions):
    half = HEAD_WIDTH // 2
    freq = rope_base ** (-(jnp.arange(half, dtype=jnp.float32) * 2.0 / HEAD_WIDTH))
    angle = positions.astype(jnp.float32)[:, None] * freq[None, :]
    cosine = jnp.cos(angle)[:, None, :]
    sine = jnp.sin(angle)[:, None, :]
    first = values_in[..., :half]
    second = values_in[..., half:]
    return jnp.concatenate(
        [first * cosine - second * sine, second * cosine + first * sine], axis=-1
    )


def attend(running, grouped_query, block_list, first_distance, seq_index, length, query_positions):
    token_count = block_list.shape[0]
    window_rows = block_list.shape[2]
    key_row_list = block_list[:, 0].reshape(token_count * window_rows, KEY_VALUE_HEADS, HEAD_WIDTH)
    value_row_list = block_list[:, 1].reshape(
        token_count * window_rows, KEY_VALUE_HEADS, HEAD_WIDTH
    )
    anchors = (seq_index - first_distance - jnp.arange(token_count, dtype=jnp.int32)) * window_rows
    key_pos = (anchors[:, None] + jnp.arange(window_rows, dtype=jnp.int32)[None, :]).reshape(-1)
    scores = jnp.einsum(
        "qgrd,kgd->grqk", grouped_query, key_row_list, preferred_element_type=jnp.float32
    ) * HEAD_WIDTH ** (-0.5)
    visible = (key_pos[None, :] <= query_positions[:, None]) & (
        query_positions[:, None] - key_pos[None, :] < WINDOW_TOKENS
    )
    visible = visible & (key_pos[None, :] >= 0) & (key_pos[None, :] < length)
    visible = visible[None, None]
    masked = jnp.where(visible, scores, negative_bound)
    old_top, old_total, old_sum = running
    new_top = jnp.maximum(old_top, jnp.max(masked, axis=-1))
    weights = jnp.where(visible, jnp.exp(masked - new_top[..., None]), 0.0)
    factor = jnp.exp(old_top - new_top)
    new_total = old_total * factor + jnp.sum(weights, axis=-1)
    product = jnp.einsum(
        "grqk,kgd->grqd",
        weights.astype(jnp.bfloat16),
        value_row_list,
        preferred_element_type=jnp.float32,
    )
    new_sum = old_sum * factor[..., None] + product
    return (new_top, new_total, new_sum)


def body(hidden_states, query_weight, key_matrix, value_matrix, context_lengths):
    token_rows = hidden_states[0]
    window_rows = token_rows.shape[0]
    q_width = QUERY_HEADS * HEAD_WIDTH
    key_value_width = KEY_VALUE_HEADS * HEAD_WIDTH
    group_size = QUERY_HEADS // KEY_VALUE_HEADS
    pieces = (
        lax.all_gather(query_weight, "dp", axis=0, tiled=True),
        lax.all_gather(key_matrix, "dp", axis=0, tiled=True),
        lax.all_gather(value_matrix, "dp", axis=0, tiled=True),
    )
    query_rows, key_row_list, value_row_list = tuple(
        (jnp.dot(token_rows, piece, preferred_element_type=jnp.float32) for piece in pieces)
    )
    seq_index = lax.axis_index("seq")
    query_positions = seq_index * window_rows + jnp.arange(window_rows, dtype=jnp.int32)
    rotated_queries = apply_rotary(
        query_rows.reshape(window_rows, QUERY_HEADS, HEAD_WIDTH), query_positions
    ).astype(jnp.bfloat16)
    rotated_keys = apply_rotary(
        key_row_list.reshape(window_rows, KEY_VALUE_HEADS, HEAD_WIDTH), query_positions
    ).astype(jnp.bfloat16)
    packed = jnp.stack(
        [rotated_keys.reshape(window_rows, key_value_width), value_row_list.astype(jnp.bfloat16)]
    )
    grouped_query = rotated_queries.reshape(window_rows, KEY_VALUE_HEADS, group_size, HEAD_WIDTH)
    length = context_lengths[0]
    running = (
        jnp.full((KEY_VALUE_HEADS, group_size, window_rows), negative_bound, jnp.float32),
        jnp.zeros((KEY_VALUE_HEADS, group_size, window_rows), jnp.float32),
        jnp.zeros((KEY_VALUE_HEADS, group_size, window_rows, HEAD_WIDTH), jnp.float32),
    )
    running = attend(running, grouped_query, packed[None], 0, seq_index, length, query_positions)
    reach = min(WINDOW_TOKENS // window_rows, lax.axis_size("seq") - 1)
    current = packed
    for distance in range(1, reach + 1):
        current = from_behind(current, "seq", 1)
        running = attend(
            running, grouped_query, current[None], distance, seq_index, length, query_positions
        )
    top_value, total, summed = running
    valid = query_positions < length
    safe = jnp.where(valid[None, None, :], total, 1.0)
    result = summed / safe[..., None]
    result = jnp.where(valid[None, None, :, None], result, 0.0)
    result = jnp.transpose(result, (2, 0, 1, 3)).reshape(window_rows, q_width)
    return result.astype(jnp.bfloat16)[None]


def solution(mesh):
    return jax.shard_map(
        body,
        mesh=mesh,
        in_specs=(P("dp", "seq", None), P("dp", None), P("dp", None), P("dp", None), P("dp")),
        out_specs=P("dp", "seq", None),
        check_vma=False,
    )
```

profile of v0, /device:TPU:131, one launch (start us, length us, event | category | flops | bytes accessed | tf_op | source)
XLA Modules:
  0.0 388.7 jit_solution(12279709319384658283)
XLA Ops:
  9.1 62.4 %all-gather.4.cloned.1.call-done = bf16[4096,512]{1,0:T(8,128)(2,1)} async-done(((bf16[256,512]{1,0:T(8,128)(2,1)}), bf16[4096,512]{1,0:T(8,128)(2,1)}) %all-gather.4.cloned.1.call-update) | async-done | bytes 4194320 | tf_op jit(solution)/shard_map/all_gather | solution.py:76
  71.5 6.4 %copy.6 = bf16[512,4096]{1,0:T(8,128)(2,1)} copy(bf16[512,4096]{0,1:T(8,128)(2,1)} %bitcast.431) | data formatting | bytes 8388608 | tf_op jit(solution)/shard_map/dot_general | solution.py:80
  77.9 3.5 fusion.58
  81.6 50.8 %all-gather.6.cloned.1.call-done = bf16[4096,512]{1,0:T(8,128)(2,1)} async-done(((bf16[256,512]{1,0:T(8,128)(2,1)}), bf16[4096,512]{1,0:T(8,128)(2,1)}) %all-gather.6.cloned.1.call-update) | async-done | bytes 4194320 | tf_op jit(solution)/shard_map/all_gather | solution.py:77
  132.5 3.4 fusion.112
  136.0 3.2 collective-permute-start
  139.2 14.5 %collective-permute-done = bf16[2,256,512]{2,1,0:T(8,128)(2,1)} collective-permute-done((bf16[2,256,512]{2,1,0:T(8,128)(2,1)S(1)}, bf16[2,256,512]{2,1,0:T(8,128)(2,1)}, u32[]{:S(2)}, u32[]{:S(2)}) %collective-permute-start) | collective-permute-done | bytes 524320 | tf_op jit(solution)/shard_map/ppermute | solution.py:19
  156.3 17.1 %collective-permute-done.1 = bf16[2,256,512]{2,1,0:T(8,128)(2,1)S(1)} collective-permute-done((bf16[2,256,512]{2,1,0:T(8,128)(2,1)}, bf16[2,256,512]{2,1,0:T(8,128)(2,1)S(1)}, u32[]{:S(2)}, u32[]{:S(2)}) %collective-permute-start.1) | collective-permute-done | bytes 524320 | tf_op jit(solution)/shard_map/ppermute | solution.py:19
  175.4 12.1 %collective-permute-done.2 = bf16[2,256,512]{2,1,0:T(8,128)(2,1)S(1)} collective-permute-done((bf16[2,256,512]{2,1,0:T(8,128)(2,1)S(1)}, bf16[2,256,512]{2,1,0:T(8,128)(2,1)S(1)}, u32[]{:S(2)}, u32[]{:S(2)}) %collective-permute-start.2) | collective-permute-done | bytes 524320 | tf_op jit(solution)/shard_map/ppermute | solution.py:19
  187.5 3.1 collective-permute-start.3
  190.7 11.7 %collective-permute-done.3 = bf16[2,256,512]{2,1,0:T(8,128)(2,1)S(1)} collective-permute-done((bf16[2,256,512]{2,1,0:T(8,128)(2,1)S(1)}, bf16[2,256,512]{2,1,0:T(8,128)(2,1)S(1)}, u32[]{:S(2)}, u32[]{:S(2)}) %collective-permute-start.3) | collective-permute-done | bytes 524320 | tf_op jit(solution)/shard_map/ppermute | solution.py:19
  202.4 2.7 collective-permute-start.4
  205.1 2.0 fusion.135
  207.1 20.8 %collective-permute-done.4 = bf16[2,256,512]{2,1,0:T(8,128)(2,1)} collective-permute-done((bf16[2,256,512]{2,1,0:T(8,128)(2,1)S(1)}, bf16[2,256,512]{2,1,0:T(8,128)(2,1)}, u32[]{:S(2)}, u32[]{:S(2)}) %collective-permute-start.4) | collective-permute-done | bytes 524320 | tf_op jit(solution)/shard_map/ppermute | solution.py:19
  227.9 1.9 collective-permute-start.5
  234.8 18.6 %collective-permute-done.5 = bf16[2,256,512]{2,1,0:T(8,128)(2,1)} collective-permute-done((bf16[2,256,512]{2,1,0:T(8,128)(2,1)}, bf16[2,256,512]{2,1,0:T(8,128)(2,1)}, u32[]{:S(2)}, u32[]{:S(2)}) %collective-permute-start.5) | collective-permute-done | bytes 524320 | tf_op jit(solution)/shard_map/ppermute | solution.py:19
  253.4 1.9 collective-permute-start.6
  262.2 16.4 %collective-permute-done.6 = bf16[2,256,512]{2,1,0:T(8,128)(2,1)} collective-permute-done((bf16[2,256,512]{2,1,0:T(8,128)(2,1)}, bf16[2,256,512]{2,1,0:T(8,128)(2,1)}, u32[]{:S(2)}, u32[]{:S(2)}) %collective-permute-start.6) | collective-permute-done | bytes 524320 | tf_op jit(solution)/shard_map/ppermute | solution.py:19
  292.1 21.0 %all-gather.8.cloned.1.call-done = bf16[4096,2048]{1,0:T(8,128)(2,1)} async-done(((bf16[256,2048]{1,0:T(8,128)(2,1)}), bf16[4096,2048]{1,0:T(8,128)(2,1)}) %all-gather.8.cloned.1.call-update) | async-done | bytes 16777232 | tf_op jit(solution)/shard_map/all_gather | solution.py:75
  313.1 20.8 %copy.8 = bf16[2048,4096]{1,0:T(8,128)(2,1)} copy(bf16[2048,4096]{0,1:T(8,128)(2,1)} %bitcast.429) | data formatting | bytes 33554432 | tf_op jit(solution)/shard_map/dot_general | solution.py:80
  333.9 8.7 %fusion.56 = f32[256,16,128]{0,2,1:T(8,128)S(1)} fusion(bf16[16,128,4096]{2,1,0:T(8,128)(2,1)} %bitcast.430, bf16[1,256,4096]{2,1,0:T(8,128)(2,1)S(1)} %copy-done), kind=kOutput, calls=%fused_computation.74 | convolution fusion | flops 4294967296 | bytes 20971520 | tf_op jit(solution)/shard_map/dot_general | solution.py:80
  354.6 2.5 fusion.43
  372.2 2.5 fusion.29
  376.5 4.1 %fusion.47 = bf16[256,4,4,128]{0,3,2,1:T(8,128)(2,1)S(1)} fusion(f32[4,4,256,128]{2,3,1,0:T(8,128)} %fusion.29, f32[4,4,256,128]{2,3,1,0:T(8,128)S(1)} %fusion.31, f32[4,4,256,128]{2,3,1,0:T(8,128)S(1)} %fusion.33, f32[4,4,256,128]{2,3,1,0:T(8,128)S(1)} %fusion.35, f32[4,4,256,128]{2,3,1,0:T(8,128)S(1)} %fusion.37, f32[4,4,256,128]{2,3,1,0:T(8,128)S(1)} %fusion.39, ...), kind=kOutput, calls=%fused_computation.57 | convolution fusion | flops 284164096 | bytes 22528256 | tf_op jit(solution)/shard_map/grqk,kgd->grqd/dot_general | solution.py:58
  (168 shorter events, 61.8 us)
Async XLA Ops:
  6.5 71.4 %copy-start = (bf16[1,256,4096]{2,1,0:T(8,128)(2,1)S(1)}, bf16[1,256,4096]{2,1,0:T(8,128)(2,1)}, u32[]{:S(2)}) copy-start(bf16[1,256,4096]{2,1,0:T(8,128)(2,1)} %param.5) | copy-start | bytes 6291460
  6.5 64.9 %all-gather.4.cloned.1.call-start = ((), (), s32[]{:S(2)}) async-start(), calls=%async_computation | async-start | bytes 4456448 | tf_op jit(solution)/shard_map/all_gather | solution.py:76
  7.3 125.2 %all-gather.6.cloned.1.call-start = ((), (), s32[]{:S(2)}) async-start(), calls=%async_computation.1 | async-start | bytes 4456448 | tf_op jit(solution)/shard_map/all_gather | solution.py:77
  8.0 305.1 %all-gather.8.cloned.1.call-start = ((), (), s32[]{:S(2)}) async-start(), calls=%async_computation.2 | async-start | bytes 17825792 | tf_op jit(solution)/shard_map/all_gather | solution.py:75
  9.1 72.3 %copy-start.17 = (f32[256,64]{0,1:T(8,128)}, f32[256,64]{0,1:T(8,128)S(1)}, u32[]{:S(2)}) copy-start(f32[256,64]{0,1:T(8,128)S(1)} %get-tuple-element.50) | copy-start | bytes 196612
  9.1 72.3 %copy-start.19 = (f32[256,64]{0,1:T(8,128)}, f32[256,64]{0,1:T(8,128)S(1)}, u32[]{:S(2)}) copy-start(f32[256,64]{0,1:T(8,128)S(1)} %get-tuple-element.51) | copy-start | bytes 196612
  136.0 17.7 %collective-permute-start = (bf16[2,256,512]{2,1,0:T(8,128)(2,1)S(1)}, bf16[2,256,512]{2,1,0:T(8,128)(2,1)}, u32[]{:S(2)}, u32[]{:S(2)}) collective-permute-start(bf16[2,256,512]{2,1,0:T(8,128)(2,1)S(1)} %get-tuple-element.44), channel_id=1, source_target_pairs={{0,1},{1,2},{2,3},{3,4},{4,5},{5,6},{6,7},{7,8},{8,9},{9,10},{10,1... | collective-permute-start | bytes 1572872 | tf_op jit(solution)/shard_map/ppermute | solution.py:19
  153.7 19.7 %collective-permute-start.1 = (bf16[2,256,512]{2,1,0:T(8,128)(2,1)}, bf16[2,256,512]{2,1,0:T(8,128)(2,1)S(1)}, u32[]{:S(2)}, u32[]{:S(2)}) collective-permute-start(bf16[2,256,512]{2,1,0:T(8,128)(2,1)} %collective-permute-done), channel_id=1, source_target_pairs={{0,1},{1,2},{2,3},{3,4},{4,5},{5,6},{6,7},{7,8},{8,9},{9,10},{10,1... | collective-permute-start | bytes 1572872 | tf_op jit(solution)/shard_map/ppermute | solution.py:19
  173.5 57.6 %copy-start.21 = (bf16[2,256,512]{2,1,0:T(8,128)(2,1)}, bf16[2,256,512]{2,1,0:T(8,128)(2,1)S(1)}, u32[]{:S(2)}) copy-start(bf16[2,256,512]{2,1,0:T(8,128)(2,1)S(1)} %collective-permute-done.1) | copy-start | bytes 1572868
  173.5 14.1 %collective-permute-start.2 = (bf16[2,256,512]{2,1,0:T(8,128)(2,1)S(1)}, bf16[2,256,512]{2,1,0:T(8,128)(2,1)S(1)}, u32[]{:S(2)}, u32[]{:S(2)}) collective-permute-start(bf16[2,256,512]{2,1,0:T(8,128)(2,1)S(1)} %collective-permute-done.1), channel_id=1, source_target_pairs={{0,1},{1,2},{2,3},{3,4},{4,5},{5,6},{6,7},{7,8},{8,9},{9,10},{10,1... | collective-permute-start | bytes 1572872 | tf_op jit(solution)/shard_map/ppermute | solution.py:19
  187.5 43.6 %copy-start.22 = (bf16[2,256,512]{2,1,0:T(8,128)(2,1)}, bf16[2,256,512]{2,1,0:T(8,128)(2,1)S(1)}, u32[]{:S(2)}) copy-start(bf16[2,256,512]{2,1,0:T(8,128)(2,1)S(1)} %collective-permute-done.2) | copy-start | bytes 1572868
  187.5 14.8 %collective-permute-start.3 = (bf16[2,256,512]{2,1,0:T(8,128)(2,1)S(1)}, bf16[2,256,512]{2,1,0:T(8,128)(2,1)S(1)}, u32[]{:S(2)}, u32[]{:S(2)}) collective-permute-start(bf16[2,256,512]{2,1,0:T(8,128)(2,1)S(1)} %collective-permute-done.2), channel_id=1, source_target_pairs={{0,1},{1,2},{2,3},{3,4},{4,5},{5,6},{6,7},{7,8},{8,9},{9,10},{10,1... | collective-permute-start | bytes 1572872 | tf_op jit(solution)/shard_map/ppermute | solution.py:19
  190.7 43.2 %copy-start.35 = (pred[256]{0:T(512)(128)(4,1)}, pred[256]{0:T(512)(128)(4,1)S(1)}, u32[]{:S(2)}) copy-start(pred[256]{0:T(512)(128)(4,1)S(1)} %get-tuple-element.82) | copy-start | bytes 772
  202.4 28.7 %copy-start.24 = (bf16[2,256,512]{2,1,0:T(8,128)(2,1)}, bf16[2,256,512]{2,1,0:T(8,128)(2,1)S(1)}, u32[]{:S(2)}) copy-start(bf16[2,256,512]{2,1,0:T(8,128)(2,1)S(1)} %collective-permute-done.3) | copy-start | bytes 1572868
  202.4 25.6 %collective-permute-start.4 = (bf16[2,256,512]{2,1,0:T(8,128)(2,1)S(1)}, bf16[2,256,512]{2,1,0:T(8,128)(2,1)}, u32[]{:S(2)}, u32[]{:S(2)}) collective-permute-start(bf16[2,256,512]{2,1,0:T(8,128)(2,1)S(1)} %collective-permute-done.3), channel_id=1, source_target_pairs={{0,1},{1,2},{2,3},{3,4},{4,5},{5,6},{6,7},{7,8},{8,9},{9,10},{10,1... | collective-permute-start | bytes 1572872 | tf_op jit(solution)/shard_map/ppermute | solution.py:19
  227.9 25.4 %collective-permute-start.5 = (bf16[2,256,512]{2,1,0:T(8,128)(2,1)}, bf16[2,256,512]{2,1,0:T(8,128)(2,1)}, u32[]{:S(2)}, u32[]{:S(2)}) collective-permute-start(bf16[2,256,512]{2,1,0:T(8,128)(2,1)} %collective-permute-done.4), channel_id=1, source_target_pairs={{0,1},{1,2},{2,3},{3,4},{4,5},{5,6},{6,7},{7,8},{8,9},{9,10},{10,1... | collective-permute-start | bytes 1572872 | tf_op jit(solution)/shard_map/ppermute | solution.py:19
  232.7 25.2 %copy-start.23 = (bf16[2,256,512]{2,1,0:T(8,128)(2,1)S(1)}, bf16[2,256,512]{2,1,0:T(8,128)(2,1)}, u32[]{:S(2)}) copy-start(bf16[2,256,512]{2,1,0:T(8,128)(2,1)} %copy-done.22) | copy-start | bytes 1572868
  253.4 25.3 %collective-permute-start.6 = (bf16[2,256,512]{2,1,0:T(8,128)(2,1)}, bf16[2,256,512]{2,1,0:T(8,128)(2,1)}, u32[]{:S(2)}, u32[]{:S(2)}) collective-permute-start(bf16[2,256,512]{2,1,0:T(8,128)(2,1)} %collective-permute-done.5), channel_id=1, source_target_pairs={{0,1},{1,2},{2,3},{3,4},{4,5},{5,6},{6,7},{7,8},{8,9},{9,10},{10,1... | collective-permute-start | bytes 1572872 | tf_op jit(solution)/shard_map/ppermute | solution.py:19
  278.7 11.8 %collective-permute-start.7 = (bf16[2,256,512]{2,1,0:T(8,128)(2,1)}, bf16[2,256,512]{2,1,0:T(8,128)(2,1)S(1)}, u32[]{:S(2)}, u32[]{:S(2)}) collective-permute-start(bf16[2,256,512]{2,1,0:T(8,128)(2,1)} %collective-permute-done.6), channel_id=1, source_target_pairs={{0,1},{1,2},{2,3},{3,4},{4,5},{5,6},{6,7},{7,8},{8,9},{9,10},{10,1... | collective-permute-start | bytes 1572872 | tf_op jit(solution)/shard_map/ppermute | solution.py:19
  333.9 8.7 %copy-start.18 = (f32[256,64]{0,1:T(8,128)S(1)}, f32[256,64]{0,1:T(8,128)}, u32[]{:S(2)}) copy-start(f32[256,64]{0,1:T(8,128)} %copy-done.17) | copy-start | bytes 196612
  333.9 8.7 %copy-start.20 = (f32[256,64]{0,1:T(8,128)S(1)}, f32[256,64]{0,1:T(8,128)}, u32[]{:S(2)}) copy-start(f32[256,64]{0,1:T(8,128)} %copy-done.19) | copy-start | bytes 196612
  354.6 3.6 copy-start.26
  372.2 3.6 copy-start.36
  376.5 5.5 %copy-start.1 = (bf16[1,256,4096]{2,1,0:T(8,128)(2,1)S(1)}, bf16[1,256,4096]{2,1,0:T(8,128)(2,1)}, u32[]{:S(2)}) copy-start(bf16[1,256,4096]{2,1,0:T(8,128)(2,1)} %param.5) | copy-start | bytes 6291460
  (25 other events, 48.3 us)
Sparse Core Ops, SparseCore 0:
  10.1 61.3 all-gather.3
  74.2 58.1 all-gather.5
  135.2 177.7 all-gather.7
where the time goes:
time: 397 us; the launch traced here: 389 us
  waiting for transfers between devices  249 us (63%)
  local copies, waits for them, and re-layouts  50.8 us (13%)
  matrix products  40.2 us (10%)
  starting transfers between devices  18.6 us (5%)
  other arithmetic  15 us (4%)
  between operations  14.9 us (4%)
    ppermute x8, waiting for transfers between devices, from_behind(): return lax.ppermute(block, axis, route)  113 us
    all_gather x1, waiting for transfers between devices, body(): lax.all_gather(key_matrix, 'dp', axis=0, tiled=True)  62.4 us
    all_gather x1, waiting for transfers between devices, body(): lax.all_gather(value_matrix, 'dp', axis=0, tiled=True)  50.8 us
    dot_general x2, local copies, waits for them, and re-layouts, body(): jnp.dot(token_rows, piece, preferred_element_type=jnp.float32)  27.2 us
    all_gather x1, waiting for transfers between devices, body(): lax.all_gather(query_weight, 'dp', axis=0, tiled=True)  21 us
    ppermute x8, starting transfers between devices, from_behind(): return lax.ppermute(block, axis, route)  18.6 us
    dot_general x9, matrix products, attend(): jnp.einsum('grqk,kgd->grqd', weights.astype(jnp.bfloat16), value_row_list...  16.5 us
    dot_general x3, matrix products, body(): jnp.dot(token_rows, piece, preferred_element_type=jnp.float32)  15.6 us
  transfers between devices with their start and end apart: 11, of which 11 were waited for; matrix products, arithmetic and copies ran while one was open for 10% of the time, Pallas kernels for 0%

commit v1 on v0

v1 whole, which is shorter than its diff:
```python
import functools

import jax
import jax.numpy as jnp
from jax import lax
from jax.experimental import pallas as pl
from jax.experimental.pallas import tpu as pltpu
from jax.sharding import PartitionSpec as P

HEAD_WIDTH = 128
WINDOW_TOKENS = 2048
SLAB = 256
SHARD = 512
SHARDS = 8
DEPTH = SHARD * SHARDS
GROUP = 4
SLOTS = WINDOW_TOKENS // SLAB + 1
LEVELS = 4
SCORE_SCALE = HEAD_WIDTH**-0.5 * 1.4426950408889634
rope_base = 10000.0
negative_bound = -1e30
MESH = pl.DeviceIdType.MESH

PIECES = ("k", "v", "q0", "q1")
SWAP, YP, YM, XB, YP_A, YM_A, YP_B, YM_B, XB_A = range(9)
PER_PIECE = 9
HALO = PER_PIECE * len(PIECES)
OUT = HALO + 4 * LEVELS
X_SWAP = OUT + 2
FLOWS = X_SWAP + 1


def rope_tables(seq):
    half = HEAD_WIDTH // 2
    positions = seq * SLAB + jnp.arange(SLAB, dtype=jnp.int32)
    freq = rope_base ** (-(jnp.arange(half, dtype=jnp.float32) * 2.0 / HEAD_WIDTH))
    angle = positions.astype(jnp.float32)[:, None] * freq[None, :]
    cosine, sine = jnp.cos(angle), jnp.sin(angle)
    return jnp.concatenate([cosine, cosine], 1), jnp.concatenate([-sine, sine], 1)


def kernel(
    x_ref, wq_ref, wk_ref, wv_ref, cos_ref, sin_ref, out_ref,
    xbuf, wk, wv, wq0, wq1, kbuf, vbuf, qbuf, stage, acc, top, total,
    send, recv, local,
):
    dp, seq = lax.axis_index("dp"), lax.axis_index("seq")
    hi, y, core = dp // 8, (dp // 2) % 4, dp % 2
    z, lo = seq // 2, seq % 2
    up, down, across = (y + 1) % 4, (y + 3) % 4, (y + 2) % 4

    def device(hi, y, core, z, lo):
        return (hi * 8 + y * 2 + core, z * 2 + lo)

    partner = device(hi, y, 1 - core, z, lo)
    y_next, y_prev = device(hi, up, core, z, lo), device(hi, down, core, z, lo)
    x_far = device(1 - hi, y, core, z, 1 - lo)
    x_near = device(hi, y, core, z, 1 - lo)
    z_next, z_prev = device(hi, y, core, (z + 1) % 8, lo), device(hi, y, core, (z + 7) % 8, lo)

    def remote(src, dst, flow, to):
        return pltpu.make_async_remote_copy(
            src_ref=src, dst_ref=dst, send_sem=send.at[flow], recv_sem=recv.at[flow],
            device_id=to, device_id_type=MESH,
        )

    def shard(g, yy):
        return g * 4 + yy

    def rows(w, s, first=0, count=SHARD):
        return w.at[pl.ds(pl.multiple_of(s * SHARD + first, 256), count)]

    def columns(ref, c, j, width):
        if ref is wq_ref:
            return ref.at[:, pl.ds(pl.multiple_of(c * 1024 + j * 512, 512), width)]
        return ref.at[:, pl.ds(pl.multiple_of(c * 256, 256), width)]

    weights = {
        "k": (wk_ref, wk, 0, 256), "v": (wv_ref, wv, 0, 256),
        "q0": (wq_ref, wq0, 0, 512), "q1": (wq_ref, wq1, 1, 512),
    }

    mine = shard(hi, y)

    class Piece:
        def __init__(self, name):
            self.index = PIECES.index(name)
            self.ref, self.w, self.j, self.width = weights[name]
            base = PER_PIECE * self.index
            w = self.w
            self.local = pltpu.make_async_copy(
                columns(self.ref, core, self.j, self.width),
                w.at[pl.ds(pl.multiple_of(mine * SHARD + core * 256, 256), 256)],
                local.at[self.index],
            )
            theirs = w.at[pl.ds(pl.multiple_of(mine * SHARD + core * 256, 256), 256)]
            ours = w.at[pl.ds(pl.multiple_of(mine * SHARD + (1 - core) * 256, 256), 256)]
            self.swap_out = remote(
                columns(self.ref, 1 - core, self.j, self.width), theirs, base + SWAP, partner
            )
            self.swap_in = remote(ours, ours, base + SWAP, partner)

            def both(flow, to, out_part, in_part):
                return (
                    remote(out_part, out_part, base + flow, to),
                    remote(in_part, in_part, base + flow, to),
                )

            own = rows(w, mine)
            far = shard(1 - hi, y)
            self.flows = {
                YP: both(YP, y_next, own, rows(w, shard(hi, down))),
                YM: both(YM, y_prev, own, rows(w, shard(hi, up))),
                XB: both(XB, x_far, own, rows(w, far)),
                YP_A: both(YP_A, y_next, rows(w, shard(hi, down), 0, 256), rows(w, shard(hi, across), 0, 256)),
                YM_A: both(YM_A, y_prev, rows(w, shard(hi, up), 256, 256), rows(w, shard(hi, across), 256, 256)),
                YP_B: both(YP_B, y_next, rows(w, far), rows(w, shard(1 - hi, down))),
                YM_B: both(YM_B, y_prev, rows(w, far), rows(w, shard(1 - hi, up))),
                XB_A: both(XB_A, x_far, rows(w, shard(hi, across)), rows(w, shard(1 - hi, across))),
            }

        def go(self, *flows):
            for f in flows:
                self.flows[f][0].start()

        def got(self, *flows):
            for f in flows:
                self.flows[f][1].wait_recv()

        def p0(self):
            self.local.wait()
            self.swap_in.wait_recv()
            self.go(XB, YP, YM)

        def p1(self):
            self.got(XB)
            self.go(YP_B, YM_B)
            self.got(YP)
            self.go(YP_A)
            self.got(YM)
            self.go(YM_A)

        def p2(self):
            self.got(YP_A, YM_A)
            self.go(XB_A)

        def p3(self):
            self.got(YP_B, YM_B, XB_A)

        def finish(self):
            self.swap_out.wait_send()
            for out, _ in self.flows.values():
                out.wait_send()

    k, v, q0, q1 = [Piece(name) for name in PIECES]

    x_local = pltpu.make_async_copy(x_ref, xbuf.at[core], local.at[4])
    k.local.start()
    x_local.start()
    for piece in (v, q0, q1):
        piece.local.start()

    barrier = pltpu.get_barrier_semaphore()
    partners = (partner, y_next, y_prev, x_far, x_near, z_next, z_prev)
    for other in partners:
        pl.semaphore_signal(barrier, inc=1, device_id=other, device_id_type=MESH)
    pl.semaphore_wait(barrier, len(partners))

    x_out = remote(x_ref, xbuf.at[core], X_SWAP, partner)
    x_in = remote(xbuf.at[1 - core], xbuf.at[1 - core], X_SWAP, partner)
    k.swap_out.start()
    x_out.start()
    for piece in (v, q0, q1):
        piece.swap_out.start()

    def rotate(values):
        return values * cos_ref[...] + pltpu.roll(values, HEAD_WIDTH // 2, 1) * sin_ref[...]

    class Halo:
        def __init__(self, which, buf):
            self.base = HALO + which * 2 * LEVELS
            self.buf = buf

        def z_send(self, level):
            return remote(self.buf.at[2 * level], self.buf.at[2 * level + 2], self.base + level, z_next)

        def near_send(self, level, step):
            return remote(self.buf.at[2 * level], self.buf.at[2 * step + 1], self.base + LEVELS + step, x_near)

        def level(self, level):
            if level > 0:
                self.z_send(level - 1).wait_recv()
            if level < LEVELS:
                self.z_send(level).start()

                @pl.when(lo == 0)
                def _():
                    self.near_send(level, level).start()

            if level > 0:

                @pl.when(lo == 1)
                def _():
                    self.near_send(level, level - 1).start()

        def near(self, step):
            self.near_send(step, step).wait_recv()

        def finish(self):
            for i in range(LEVELS):
                self.z_send(i).wait_send()
                self.near_send(i, i).wait_send()

    halo_k, halo_v = Halo(0, kbuf), Halo(1, vbuf)

    def project_k():
        @pl.loop(0, 2)
        def _(ctx):
            full = jnp.dot(xbuf[ctx], wk[...], preferred_element_type=jnp.float32)
            for j in range(2):
                head = full[:, j * HEAD_WIDTH : (j + 1) * HEAD_WIDTH]
                kbuf[0, ctx, :, j * HEAD_WIDTH : (j + 1) * HEAD_WIDTH] = rotate(head).astype(jnp.bfloat16)

    def project_v():
        @pl.loop(0, 2)
        def _(ctx):
            full = jnp.dot(xbuf[ctx], wv[...], preferred_element_type=jnp.float32)
            vbuf[0, ctx] = full.astype(jnp.bfloat16)

    def project_q(j, w):
        @pl.loop(0, 2)
        def _(ctx):
            full = jnp.dot(xbuf[ctx], w[...], preferred_element_type=jnp.float32)
            for h in range(GROUP):
                head = full[:, h * HEAD_WIDTH : (h + 1) * HEAD_WIDTH]
                qbuf[j, ctx, h * SLAB : (h + 1) * SLAB] = rotate(head).astype(jnp.bfloat16)

    tall = GROUP * SLAB

    def attend(j, ctx):
        lanes = slice(j * HEAD_WIDTH, (j + 1) * HEAD_WIDTH)
        contract = (((1,), (1,)), ((), ()))

        def scores(d):
            return lax.dot_general(
                qbuf[j, ctx], kbuf[d, ctx, :, lanes], contract, preferred_element_type=jnp.float32
            )

        def fold(p):
            return p[:, :128] + p[:, 128:]

        row = lax.broadcasted_iota(jnp.int32, (tall, SLAB), 0) % SLAB
        col = lax.broadcasted_iota(jnp.int32, (tall, SLAB), 1)

        s = jnp.where(col <= row, scores(0), negative_bound)
        m = jnp.max(s, axis=1, keepdims=True)
        p = jnp.exp2((s - m) * SCORE_SCALE)
        top[...] = jnp.broadcast_to(m, (tall, 128))
        total[...] = fold(p)
        acc[...] = jnp.dot(p.astype(jnp.bfloat16), vbuf[0, ctx, :, lanes], preferred_element_type=jnp.float32)

        def update(d, masked):
            s = scores(d)
            if masked:
                s = jnp.where(col > row, s, negative_bound)
            old = top[...]
            m = jnp.maximum(old, jnp.max(s, axis=1, keepdims=True))
            factor = jnp.exp2((old - m) * SCORE_SCALE)
            p = jnp.exp2((s - jnp.concatenate([m, m], 1)) * SCORE_SCALE)
            top[...] = m
            total[...] = total[...] * factor + fold(p)
            acc[...] = acc[...] * factor + jnp.dot(
                p.astype(jnp.bfloat16), vbuf[d, ctx, :, lanes], preferred_element_type=jnp.float32
            )

        lax.fori_loop(1, jnp.minimum(seq, SLOTS - 2) + 1, lambda d, c: (update(d, False), c)[1], 0)

        @pl.when(seq >= SLOTS - 1)
        def _():
            update(SLOTS - 1, True)

        result = acc[...] / jnp.sum(total[...], axis=1, keepdims=True)
        for h in range(GROUP):
            stage[j, ctx, :, h * HEAD_WIDTH : (h + 1) * HEAD_WIDTH] = result[
                h * SLAB : (h + 1) * SLAB
            ].astype(jnp.bfloat16)

    def out_columns(j):
        return out_ref.at[:, pl.ds(pl.multiple_of(core * 1024 + j * 512, 512), 512)]

    def out_arrive(j):
        theirs = out_ref.at[:, pl.ds(pl.multiple_of((1 - core) * 1024 + j * 512, 512), 512)]
        return remote(stage.at[j, core], theirs, OUT + j, partner)

    def out_local(j):
        return pltpu.make_async_copy(stage.at[j, core], out_columns(j), local.at[5 + j])

    def out_remote(j):
        return remote(stage.at[j, 1 - core], out_columns(j), OUT + j, partner)

    k.p0()
    k.p1()
    k.p2()
    v.p0()
    x_local.wait()
    x_in.wait_recv()
    k.p3()
    project_k()
    halo_k.level(0)
    v.p1()
    halo_k.level(1)
    v.p2()
    q0.p0()
    v.p3()
    project_v()
    halo_v.level(0)
    halo_k.level(2)
    halo_k.level(3)
    q0.p1()
    halo_v.level(1)
    halo_k.level(4)
    halo_v.level(2)
    q0.p2()
    q1.p0()
    halo_v.level(3)
    q0.p3()
    project_q(0, wq0)
    halo_v.level(4)
    for step in range(LEVELS):
        halo_k.near(step)
        halo_v.near(step)
    attend(0, 1 - core)
    q1.p1()
    attend(0, core)
    out_remote(0).start()
    out_local(0).start()
    q1.p2()
    q1.p3()
    project_q(1, wq1)
    attend(1, 1 - core)
    out_remote(1).start()
    attend(1, core)
    out_local(1).start()

    for piece in (k, v, q0, q1):
        piece.finish()
    x_out.wait_send()
    halo_k.finish()
    halo_v.finish()
    for j in range(2):
        out_local(j).wait()
        out_remote(j).wait_send()
        out_arrive(j).wait_recv()


def body(hidden_states, query_weight, key_matrix, value_matrix, context_lengths):
    x = hidden_states[0]
    seq = lax.axis_index("seq")
    cosine, sine = rope_tables(seq)
    any_space = pl.BlockSpec(memory_space=pl.ANY)
    vmem = pl.BlockSpec(memory_space=pltpu.VMEM)
    bf16, f32 = jnp.bfloat16, jnp.float32
    tall = GROUP * SLAB
    attended = pl.pallas_call(
        kernel,
        out_shape=jax.ShapeDtypeStruct((SLAB, 2048), bf16),
        in_specs=[any_space] * 4 + [vmem] * 2,
        out_specs=any_space,
        scratch_shapes=[
            pltpu.VMEM((2, SLAB, DEPTH), bf16),
            pltpu.VMEM((DEPTH, 256), bf16),
            pltpu.VMEM((DEPTH, 256), bf16),
            pltpu.VMEM((DEPTH, 512), bf16),
            pltpu.VMEM((DEPTH, 512), bf16),
            pltpu.VMEM((SLOTS, 2, SLAB, 256), bf16),
            pltpu.VMEM((SLOTS, 2, SLAB, 256), bf16),
            pltpu.VMEM((2, 2, tall, HEAD_WIDTH), bf16),
            pltpu.VMEM((2, 2, SLAB, 512), bf16),
            pltpu.VMEM((tall, HEAD_WIDTH), f32),
            pltpu.VMEM((tall, HEAD_WIDTH), f32),
            pltpu.VMEM((tall, HEAD_WIDTH), f32),
            pltpu.SemaphoreType.DMA((FLOWS,)),
            pltpu.SemaphoreType.DMA((FLOWS,)),
            pltpu.SemaphoreType.DMA((7,)),
        ],
        compiler_params=pltpu.CompilerParams(
            collective_id=0, has_side_effects=True, vmem_limit_bytes=56 * 2**20
        ),
        name="gather_project_attend",
    )(x, query_weight, key_matrix, value_matrix, cosine, sine)
    positions = seq * SLAB + jnp.arange(SLAB, dtype=jnp.int32)
    valid = positions < context_lengths[0]
    return jnp.where(valid[:, None], attended, jnp.zeros_like(attended))[None]


def solution(mesh):
    return jax.shard_map(
        body,
        mesh=mesh,
        in_specs=(P("dp", "seq", None), P("dp", None), P("dp", None), P("dp", None), P("dp")),
        out_specs=P("dp", "seq", None),
        check_vma=False,
    )
```

time: 397 us -> 152 us (0.38)
  the two profiles are of different devices: /device:TPU:131 before, /device:TPU:138 now
where the time goes in v1:
time: 152 us
  Pallas kernels  148 us (97%)
  other arithmetic  3.73 us (2%)
    pallas_call x1, Pallas kernels, body(): pl.pallas_call(kernel, out_shape=jax.ShapeDtypeStruct((SLAB, 2048), bf16)...  148 us

profile of v1, /device:TPU:138, one launch (start us, length us, event | category | flops | bytes accessed | tf_op | source)
XLA Modules:
  0.0 152.2 jit_solution(6903165596639509545)
XLA Ops:
  0.7 0.5 fusion
  1.2 0.8 pad_maximum_fusion
  2.1 147.8 %gather_project_attend.1 = bf16[256,2048]{1,0:T(8,128)(2,1)} custom-call(bf16[256,4096]{1,0:T(8,128)(2,1)} %bitcast.5, bf16[256,2048]{1,0:T(8,128)(2,1)} %wq_ref.1, bf16[256,512]{1,0:T(8,128)(2,1)} %wk_ref.1, bf16[256,512]{1,0:T(8,128)(2,1)} %wv_ref.1, f32[256,128]{1,0:T(8,128)} %get-tuple-element.8.cos_ref, f32[256,128]{1,0:T(8,128)} %get-tuple-element.9.sin_ref), custom_call_target="tpu_custom_call" | custom-call | tf_op jit(solution)/shard_map/gather_project_attend/pallas_call | solution.py:364
  149.9 2.3 %select_bitcast_fusion = bf16[1,256,2048]{2,1,0:T(8,128)(2,1)} fusion(bf16[256,2048]{1,0:T(8,128)(2,1)} %gather_project_attend.1, pred[256]{0:T(512)(128)(4,1)S(1)} %fusion.2), kind=kLoop, calls=%fused_computation | loop fusion | flops 524288 | bytes 2097408 | tf_op jit(solution)/shard_map/broadcast_in_dim | solution.py:393
  (3 shorter events, 0.0 us)

commit v2 on v1

v2 whole, which is shorter than its diff:
```python
import functools

import jax
import jax.numpy as jnp
from jax import lax
from jax.experimental import pallas as pl
from jax.experimental.pallas import tpu as pltpu
from jax.sharding import PartitionSpec as P

HEAD_WIDTH = 128
SLAB = 256
PAIR = 2 * SLAB
SHARD = 512
SHARDS = 8
DEPTH = SHARD * SHARDS
LEVELS = 4
TALL = 4 * SLAB
X_CHUNKS = 4
SCORE_SCALE = HEAD_WIDTH**-0.5 * 1.4426950408889634
rope_base = 10000.0
negative_bound = -1e30
MESH = pl.DeviceIdType.MESH

PIECES = ("k", "v", "qa", "qb")
SWAP, YP, YM, XB, YP_A, YM_A, YP_B, YM_B, XB_A = range(9)
PER_PIECE = 9
HALO = PER_PIECE * len(PIECES)
PER_HALO = LEVELS + 1
OUT = HALO + 2 * PER_HALO
PER_OUT = 3
X_SWAP = OUT + 2 * PER_OUT
X_NEAR = X_SWAP + 1
X_FORWARD = X_NEAR + X_CHUNKS
FLOWS = X_FORWARD + 1


def rope_tables(z):
    half = HEAD_WIDTH // 2
    positions = z * PAIR + jnp.arange(PAIR, dtype=jnp.int32)
    freq = rope_base ** (-(jnp.arange(half, dtype=jnp.float32) * 2.0 / HEAD_WIDTH))
    angle = positions.astype(jnp.float32)[:, None] * freq[None, :]
    cosine, sine = jnp.cos(angle), jnp.sin(angle)
    return (
        jnp.concatenate([cosine, cosine], 1).reshape(2, SLAB, HEAD_WIDTH),
        jnp.concatenate([-sine, sine], 1).reshape(2, SLAB, HEAD_WIDTH),
    )


def kernel(
    x_ref, wq_ref, wk_ref, wv_ref, cos_ref, sin_ref, out_ref,
    xbuf, wk, wv, wqa, wqb, khead, vhead, kbuf, vbuf, qbuf, stage, acc, top, total,
    send, recv, local,
):
    dp, seq = lax.axis_index("dp"), lax.axis_index("seq")
    hi, y, core = dp // 8, (dp // 2) % 4, dp % 2
    z, lo = seq // 2, seq % 2
    pick = (lo + hi) % 2
    up, down, across = (y + 1) % 4, (y + 3) % 4, (y + 2) % 4

    def device(hi, y, core, z, lo):
        return (hi * 8 + y * 2 + core, z * 2 + lo)

    partner = device(hi, y, 1 - core, z, lo)
    y_next, y_prev = device(hi, up, core, z, lo), device(hi, down, core, z, lo)
    x_far = device(1 - hi, y, core, z, 1 - lo)
    x_near = device(hi, y, core, z, 1 - lo)
    x_diag = device(hi, y, 1 - core, z, 1 - lo)
    z_next, z_prev = device(hi, y, core, (z + 1) % 8, lo), device(hi, y, core, (z + 7) % 8, lo)

    def remote(src, dst, flow, to):
        return pltpu.make_async_remote_copy(
            src_ref=src, dst_ref=dst, send_sem=send.at[flow], recv_sem=recv.at[flow],
            device_id=to, device_id_type=MESH,
        )

    def shard(g, yy):
        return g * 4 + yy

    def rows(w, s, first=0, count=SHARD):
        return w.at[pl.ds(pl.multiple_of(s * SHARD + first, 256), count)]

    def columns(name, c):
        if name == "k":
            return wk_ref.at[:, pl.ds(pl.multiple_of(c * 256, 256), 256)]
        if name == "v":
            return wv_ref.at[:, pl.ds(pl.multiple_of(c * 256, 256), 256)]
        first = (2 * c + pick) * 512 + (256 if name == "qb" else 0)
        return wq_ref.at[:, pl.ds(pl.multiple_of(first, 256), 256)]

    buffers = {"k": wk, "v": wv, "qa": wqa, "qb": wqb}
    mine = shard(hi, y)

    class Piece:
        def __init__(self, name):
            self.index = PIECES.index(name)
            w = self.w = buffers[name]
            base = PER_PIECE * self.index
            theirs = w.at[pl.ds(pl.multiple_of(mine * SHARD + core * 256, 256), 256)]
            ours = w.at[pl.ds(pl.multiple_of(mine * SHARD + (1 - core) * 256, 256), 256)]
            self.local = pltpu.make_async_copy(columns(name, core), theirs, local.at[self.index])
            self.swap_out = remote(columns(name, 1 - core), theirs, base + SWAP, partner)
            self.swap_in = remote(ours, ours, base + SWAP, partner)

            def both(flow, to, out_part, in_part):
                return (
                    remote(out_part, out_part, base + flow, to),
                    remote(in_part, in_part, base + flow, to),
                )

            own = rows(w, mine)
            far = shard(1 - hi, y)
            self.flows = {
                YP: both(YP, y_next, own, rows(w, shard(hi, down))),
                YM: both(YM, y_prev, own, rows(w, shard(hi, up))),
                XB: both(XB, x_far, own, rows(w, far)),
                YP_A: both(YP_A, y_next, rows(w, shard(hi, down), 0, 256), rows(w, shard(hi, across), 0, 256)),
                YM_A: both(YM_A, y_prev, rows(w, shard(hi, up), 256, 256), rows(w, shard(hi, across), 256, 256)),
                YP_B: both(YP_B, y_next, rows(w, far), rows(w, shard(1 - hi, down))),
                YM_B: both(YM_B, y_prev, rows(w, far), rows(w, shard(1 - hi, up))),
                XB_A: both(XB_A, x_far, rows(w, shard(hi, across)), rows(w, shard(1 - hi, across))),
            }

        def go(self, *flows):
            for f in flows:
                self.flows[f][0].start()

        def got(self, *flows):
            for f in flows:
                self.flows[f][1].wait_recv()

        def p0(self):
            self.local.wait()
            self.swap_in.wait_recv()
            self.go(XB, YP, YM)

        def p1(self):
            self.got(YP)
            self.go(YP_A)
            self.got(YM)
            self.go(YM_A)
            self.got(XB)
            self.go(YP_B, YM_B)

        def p2(self):
            self.got(YP_A, YM_A)
            self.go(XB_A)

        def p3(self):
            self.got(YP_B, YM_B, XB_A)

        def finish(self):
            self.swap_out.wait_send()
            for out, _ in self.flows.values():
                out.wait_send()

    k, v, qa, qb = [Piece(name) for name in PIECES]
    pieces = (k, v, qa, qb)

    x_local = pltpu.make_async_copy(x_ref, xbuf.at[lo, core], local.at[4])
    for piece in pieces:
        piece.local.start()
    x_local.start()

    barrier = pltpu.get_barrier_semaphore()
    partners = (partner, y_next, y_prev, x_far, x_near, x_diag, z_next, z_prev)
    for other in partners:
        pl.semaphore_signal(barrier, inc=1, device_id=other, device_id_type=MESH)
    pl.semaphore_wait(barrier, len(partners))

    x_out = remote(x_ref, xbuf.at[lo, core], X_SWAP, partner)
    x_in = remote(xbuf.at[lo, 1 - core], xbuf.at[lo, 1 - core], X_SWAP, partner)

    def x_near_out(i):
        part = pl.ds(i * (SLAB // X_CHUNKS), SLAB // X_CHUNKS)
        return remote(x_ref.at[part], xbuf.at[lo, core, part], X_NEAR + i, x_near)

    def x_near_in(i):
        part = pl.ds(i * (SLAB // X_CHUNKS), SLAB // X_CHUNKS)
        there = xbuf.at[1 - lo, core, part]
        return remote(there, there, X_NEAR + i, x_near)

    x_forward_out = remote(xbuf.at[1 - lo, core], xbuf.at[1 - lo, core], X_FORWARD, partner)
    x_forward_in = remote(xbuf.at[1 - lo, 1 - core], xbuf.at[1 - lo, 1 - core], X_FORWARD, partner)

    for piece in pieces:
        piece.swap_out.start()
    x_out.start()

    def rotate(values, which):
        return values * cos_ref[which] + pltpu.roll(values, HEAD_WIDTH // 2, 1) * sin_ref[which]

    class Halo:
        def __init__(self, which, heads, buf):
            self.base = HALO + which * PER_HALO
            self.heads, self.buf = heads, buf
            self.near_out = remote(heads.at[1 - pick], buf.at[0, :, lo], self.base + LEVELS, x_near)
            there = buf.at[0, :, 1 - lo]
            self.near_in = remote(there, there, self.base + LEVELS, x_near)

        def near(self):
            self.near_out.start()
            self.buf[0, :, lo] = self.heads[pick]

        def z_send(self, level):
            return remote(self.buf.at[level], self.buf.at[level + 1], self.base + level, z_next)

        def level(self, level):
            if level == 0:
                self.near_in.wait_recv()
            else:
                self.z_send(level - 1).wait_recv()
            if level < LEVELS:
                self.z_send(level).start()

        def finish(self):
            self.near_out.wait_send()
            for i in range(LEVELS):
                self.z_send(i).wait_send()

    halo_k, halo_v = Halo(0, khead, kbuf), Halo(1, vhead, vbuf)

    def project_k():
        @pl.loop(0, 2)
        def _(ctx):
            full = jnp.dot(xbuf[lo, ctx], wk[...], preferred_element_type=jnp.float32)
            for j in range(2):
                head = full[:, j * HEAD_WIDTH : (j + 1) * HEAD_WIDTH]
                khead[j, ctx] = rotate(head, lo).astype(jnp.bfloat16)

    def project_v():
        @pl.loop(0, 2)
        def _(ctx):
            full = jnp.dot(xbuf[lo, ctx], wv[...], preferred_element_type=jnp.float32)
            for j in range(2):
                vhead[j, ctx] = full[:, j * HEAD_WIDTH : (j + 1) * HEAD_WIDTH].astype(jnp.bfloat16)

    def project_q(half, w, side):
        @pl.loop(0, 2)
        def _(ctx):
            full = jnp.dot(xbuf[side, ctx], w[...], preferred_element_type=jnp.float32)
            for h in range(2):
                head = full[:, h * HEAD_WIDTH : (h + 1) * HEAD_WIDTH]
                first = pl.multiple_of(side * PAIR + h * SLAB, SLAB)
                qbuf[half, ctx, pl.ds(first, SLAB)] = rotate(head, side).astype(jnp.bfloat16)

    def scores(queries, keys):
        return lax.dot_general(
            queries, keys, (((1,), (1,)), ((), ())), preferred_element_type=jnp.float32
        )

    def fold(p):
        return sum(p[:, i : i + 128] for i in range(0, p.shape[1], 128))

    def visible(side, first_key, shape, newest):
        token = lax.broadcasted_iota(jnp.int32, shape, 0) % SLAB + side * SLAB
        key = lax.broadcasted_iota(jnp.int32, shape, 1) + first_key
        return key <= token if newest else key > token

    def begin(half, ctx):
        for side in range(2):
            part = slice(side * PAIR, (side + 1) * PAIR)
            count = (side + 1) * SLAB
            keys = kbuf[0, ctx].reshape(PAIR, HEAD_WIDTH)[:count]
            values = vbuf[0, ctx].reshape(PAIR, HEAD_WIDTH)[:count]
            s = scores(qbuf[half, ctx, part], keys)
            s = jnp.where(visible(side, 0, s.shape, True), s, negative_bound)
            m = jnp.max(s, axis=1, keepdims=True)
            p = jnp.exp2((s - m) * SCORE_SCALE)
            top[half, ctx, part] = jnp.broadcast_to(m, (PAIR, 128))
            total[half, ctx, part] = fold(p)
            acc[half, ctx, part] = jnp.dot(
                p.astype(jnp.bfloat16), values, preferred_element_type=jnp.float32
            )

    def update(half, ctx, part, s, values):
        old = top[half, ctx, part]
        m = jnp.maximum(old, jnp.max(s, axis=1, keepdims=True))
        factor = jnp.exp2((old - m) * SCORE_SCALE)
        p = jnp.exp2((s - jnp.concatenate([m] * (s.shape[1] // 128), 1)) * SCORE_SCALE)
        top[half, ctx, part] = m
        total[half, ctx, part] = total[half, ctx, part] * factor + fold(p)
        acc[half, ctx, part] = acc[half, ctx, part] * factor + jnp.dot(
            p.astype(jnp.bfloat16), values, preferred_element_type=jnp.float32
        )

    def middle(half, ctx, level):
        keys = kbuf[level, ctx].reshape(PAIR, HEAD_WIDTH)
        values = vbuf[level, ctx].reshape(PAIR, HEAD_WIDTH)
        update(half, ctx, slice(0, TALL), scores(qbuf[half, ctx], keys), values)

    def oldest(half, ctx):
        for side in range(2):
            part = slice(side * PAIR, (side + 1) * PAIR)
            first = side * SLAB
            keys = kbuf[LEVELS, ctx].reshape(PAIR, HEAD_WIDTH)[first:]
            values = vbuf[LEVELS, ctx].reshape(PAIR, HEAD_WIDTH)[first:]
            s = scores(qbuf[half, ctx, part], keys)
            s = jnp.where(visible(side, first, s.shape, False), s, negative_bound)
            update(half, ctx, part, s, values)

    def attend(half, first, last):
        @pl.loop(0, 2)
        def _(ctx):
            if first == 0:
                begin(half, ctx)
            lax.fori_loop(
                max(first, 1), jnp.minimum(z, min(last, LEVELS - 1)) + 1,
                lambda level, c: (middle(half, ctx, level), c)[1], 0,
            )
            if last == LEVELS:

                @pl.when(z >= LEVELS)
                def _():
                    oldest(half, ctx)

                result = acc[half, ctx] / jnp.sum(total[half, ctx], axis=1, keepdims=True)
                for side in range(2):
                    for h in range(2):
                        first_row = side * PAIR + h * SLAB
                        stage[half, side, ctx, :, h * HEAD_WIDTH : (h + 1) * HEAD_WIDTH] = result[
                            first_row : first_row + SLAB
                        ].astype(jnp.bfloat16)

    def out_columns(half, head):
        return out_ref.at[:, pl.ds(pl.multiple_of(head * 512 + half * 256, 256), 256)]

    head = 2 * core + pick

    def out_flows(half):
        base = OUT + half * PER_OUT
        dst = out_columns(half, head)
        return (
            (remote(stage.at[half, 1 - lo, core], dst, base, x_near), 2 * core + 1 - pick),
            (remote(stage.at[half, 1 - lo, 1 - core], dst, base + 1, x_diag), 2 * (1 - core) + 1 - pick),
            (remote(stage.at[half, lo, 1 - core], dst, base + 2, partner), 2 * (1 - core) + pick),
        )

    def out_local(half):
        return pltpu.make_async_copy(stage.at[half, lo, core], out_columns(half, head), local.at[5 + half])

    def out_start(half):
        for flow, _ in out_flows(half):
            flow.start()
        out_local(half).start()

    def out_finish(half):
        out_local(half).wait()
        for i, (flow, other) in enumerate(out_flows(half)):
            flow.wait_send()
            landed = out_columns(half, other)
            remote(landed, landed, OUT + half * PER_OUT + i, partner).wait_recv()

    k.p0()
    x_near_out(0).start()
    x_near_out(1).start()
    k.p1()
    v.p0()
    k.p2()
    x_local.wait()
    x_in.wait_recv()
    k.p3()
    project_k()
    halo_k.near()
    v.p1()
    qa.p0()
    halo_k.level(0)
    x_near_out(2).start()
    v.p2()
    halo_k.level(1)
    v.p3()
    project_v()
    halo_v.near()
    halo_k.level(2)
    qa.p1()
    qb.p0()
    halo_v.level(0)
    x_near_out(3).start()
    qa.p2()
    halo_k.level(3)
    qa.p3()
    project_q(0, wqa, lo)
    halo_v.level(1)
    qb.p1()
    for i in range(X_CHUNKS):
        x_near_in(i).wait_recv()
    x_forward_out.start()
    halo_k.level(4)
    qb.p2()
    x_forward_in.wait_recv()
    project_q(0, wqa, 1 - lo)
    halo_v.level(2)
    attend(0, 0, 1)
    qb.p3()
    halo_v.level(3)
    project_q(1, wqb, lo)
    project_q(1, wqb, 1 - lo)
    attend(1, 0, 2)
    halo_v.level(4)
    attend(0, 2, 4)
    out_start(0)
    attend(1, 3, 4)
    out_start(1)

    for piece in pieces:
        piece.finish()
    x_out.wait_send()
    for i in range(X_CHUNKS):
        x_near_out(i).wait_send()
    x_forward_out.wait_send()
    halo_k.finish()
    halo_v.finish()
    for half in range(2):
        out_finish(half)


def body(hidden_states, query_weight, key_matrix, value_matrix, context_lengths):
    x = hidden_states[0]
    seq = lax.axis_index("seq")
    cosine, sine = rope_tables(seq // 2)
    any_space = pl.BlockSpec(memory_space=pl.ANY)
    vmem = pl.BlockSpec(memory_space=pltpu.VMEM)
    bf16, f32 = jnp.bfloat16, jnp.float32
    attended = pl.pallas_call(
        kernel,
        out_shape=jax.ShapeDtypeStruct((SLAB, 2048), bf16),
        in_specs=[any_space] * 4 + [vmem] * 2,
        out_specs=any_space,
        scratch_shapes=[
            pltpu.VMEM((2, 2, SLAB, DEPTH), bf16),
            pltpu.VMEM((DEPTH, 256), bf16),
            pltpu.VMEM((DEPTH, 256), bf16),
            pltpu.VMEM((DEPTH, 256), bf16),
            pltpu.VMEM((DEPTH, 256), bf16),
            pltpu.VMEM((2, 2, SLAB, HEAD_WIDTH), bf16),
            pltpu.VMEM((2, 2, SLAB, HEAD_WIDTH), bf16),
            pltpu.VMEM((LEVELS + 1, 2, 2, SLAB, HEAD_WIDTH), bf16),
            pltpu.VMEM((LEVELS + 1, 2, 2, SLAB, HEAD_WIDTH), bf16),
            pltpu.VMEM((2, 2, TALL, HEAD_WIDTH), bf16),
            pltpu.VMEM((2, 2, 2, SLAB, 256), bf16),
            pltpu.VMEM((2, 2, TALL, HEAD_WIDTH), f32),
            pltpu.VMEM((2, 2, TALL, HEAD_WIDTH), f32),
            pltpu.VMEM((2, 2, TALL, HEAD_WIDTH), f32),
            pltpu.SemaphoreType.DMA((FLOWS,)),
            pltpu.SemaphoreType.DMA((FLOWS,)),
            pltpu.SemaphoreType.DMA((7,)),
        ],
        compiler_params=pltpu.CompilerParams(
            collective_id=0, has_side_effects=True, vmem_limit_bytes=56 * 2**20
        ),
        name="gather_project_attend",
    )(x, query_weight, key_matrix, value_matrix, cosine, sine)
    positions = seq * SLAB + jnp.arange(SLAB, dtype=jnp.int32)
    valid = positions < context_lengths[0]
    return jnp.where(valid[:, None], attended, jnp.zeros_like(attended))[None]


def solution(mesh):
    return jax.shard_map(
        body,
        mesh=mesh,
        in_specs=(P("dp", "seq", None), P("dp", None), P("dp", None), P("dp", None), P("dp")),
        out_specs=P("dp", "seq", None),
        check_vma=False,
    )
```

time: 152 us -> 109 us (0.72)
  the two profiles are of different devices: /device:TPU:138 before, /device:TPU:161 now
where the time goes in v2:
time: 109 us
  Pallas kernels  104 us (95%)
  other arithmetic  4.37 us (4%)
    pallas_call x1, Pallas kernels, body(): pl.pallas_call(kernel, out_shape=jax.ShapeDtypeStruct((SLAB, 2048), bf16)...  104 us
    broadcast_in_dim x1, other arithmetic, body(): return jnp.where(valid[:, None], attended, jnp.zeros_like(attended))[None]  2.34 us

profile of v2, /device:TPU:161, one launch (start us, length us, event | category | flops | bytes accessed | tf_op | source)
XLA Modules:
  0.0 109.0 jit_solution(7040932209979691913)
XLA Ops:
  0.7 1.0 fusion
  1.7 1.0 pad_maximum_fusion
  2.7 103.9 %gather_project_attend.1 = bf16[256,2048]{1,0:T(8,128)(2,1)} custom-call(bf16[256,4096]{1,0:T(8,128)(2,1)} %bitcast.5, bf16[256,2048]{1,0:T(8,128)(2,1)} %wq_ref.1, bf16[256,512]{1,0:T(8,128)(2,1)} %wk_ref.1, bf16[256,512]{1,0:T(8,128)(2,1)} %wv_ref.1, f32[2,256,128]{2,1,0:T(8,128)} %get-tuple-element.8.cos_ref, f32[2,256,128]{2,1,0:T(8,128)} %get-tuple-element.9.sin_ref), custom_call_target="tpu_custom_call" | custom-call | tf_op jit(solution)/shard_map/gather_project_attend/pallas_call | solution.py:423
  106.6 2.3 %select_bitcast_fusion = bf16[1,256,2048]{2,1,0:T(8,128)(2,1)} fusion(bf16[256,2048]{1,0:T(8,128)(2,1)} %gather_project_attend.1, pred[256]{0:T(512)(128)(4,1)S(1)} %add_compare_fusion), kind=kLoop, calls=%fused_computation | loop fusion | flops 524288 | bytes 2097408 | tf_op jit(solution)/shard_map/broadcast_in_dim | solution.py:454
  (3 shorter events, 0.0 us)

commit v3 on v2

v3 whole, which is shorter than its diff:
```python
import functools

import jax
import jax.numpy as jnp
from jax import lax
from jax.experimental import pallas as pl
from jax.experimental.pallas import tpu as pltpu
from jax.sharding import PartitionSpec as P

HEAD_WIDTH = 128
SLAB = 256
PAIR = 2 * SLAB
SHARD = 512
SHARDS = 8
DEPTH = SHARD * SHARDS
LEVELS = 4
GROUP = 4
TALL = GROUP * SLAB
X_CHUNKS = 8
SCORE_SCALE = HEAD_WIDTH**-0.5 * 1.4426950408889634
LOG_ROPE_BASE = 9.210340371976184
negative_bound = -1e30
MESH = pl.DeviceIdType.MESH

PIECES = ("k", "v", "qa", "qb")
FLOW_NAMES = (
    "up0", "up1", "down1", "down0", "far0", "far1", "up_near", "down_near",
    "up_far0", "down_far0", "up_far1", "down_far1", "far_across0", "far_across1",
)
SHARD_NAMES = ("below", "above", "opposite", "far", "far_below", "far_above", "far_opposite")
PER_PIECE = 1 + len(FLOW_NAMES) + len(SHARD_NAMES)
HALO = PER_PIECE * len(PIECES)
PER_HALO = LEVELS + 2
OUT = HALO + 4 * PER_HALO
PER_OUT = 3
X_SWAP = OUT + PER_OUT
X_NEAR = X_SWAP + 1
X_FORWARD = X_NEAR + X_CHUNKS
FLOWS = X_FORWARD + 2


def kernel(
    x_ref, wq_ref, wk_ref, wv_ref, out_ref,
    xbuf, wk, wv, wqa, wqb, khead, vhead, kbuf, vbuf, qbuf, stage, acc, top, total, cos_ref, sin_ref,
    send, recv, local,
):
    dp, seq = lax.axis_index("dp"), lax.axis_index("seq")
    hi, y, core = dp // 8, (dp // 2) % 4, dp % 2
    z, lo = seq // 2, seq % 2
    pick = (lo + hi) % 2
    up, down, across = (y + 1) % 4, (y + 3) % 4, (y + 2) % 4

    def device(hi, y, core, z, lo):
        return (hi * 8 + y * 2 + core, z * 2 + lo)

    partner = device(hi, y, 1 - core, z, lo)
    y_next, y_prev = device(hi, up, core, z, lo), device(hi, down, core, z, lo)
    x_far = device(1 - hi, y, core, z, 1 - lo)
    x_near = device(hi, y, core, z, 1 - lo)
    x_diag = device(hi, y, 1 - core, z, 1 - lo)
    z_next, z_prev = device(hi, y, core, (z + 1) % 8, lo), device(hi, y, core, (z + 7) % 8, lo)

    def remote(src, dst, flow, to):
        return pltpu.make_async_remote_copy(
            src_ref=src, dst_ref=dst, send_sem=send.at[flow], recv_sem=recv.at[flow],
            device_id=to, device_id_type=MESH,
        )

    def shard(g, yy):
        return g * 4 + yy

    def columns(name, c):
        if name == "k":
            return wk_ref.at[:, pl.ds(pl.multiple_of(c * 256, 256), 256)]
        if name == "v":
            return wv_ref.at[:, pl.ds(pl.multiple_of(c * 256, 256), 256)]
        first = (2 * c + pick) * 512 + (256 if name == "qb" else 0)
        return wq_ref.at[:, pl.ds(pl.multiple_of(first, 256), 256)]

    buffers = {"k": wk, "v": wv, "qa": wqa, "qb": wqb}
    mine = shard(hi, y)

    parity = z % 2

    class Piece:
        def __init__(self, name, along_z=None):
            self.index = PIECES.index(name)
            w = buffers[name]
            base = PER_PIECE * self.index

            def block(s, first, count, lanes):
                rows = pl.ds(pl.multiple_of(s * SHARD + first, 256), count)
                return w.at[rows, lanes]

            everything = pl.ds(0, 256)
            theirs = block(mine, core * 256, 256, everything)
            ours = block(mine, (1 - core) * 256, 256, everything)
            self.local = pltpu.make_async_copy(columns(name, core), theirs, local.at[self.index])
            self.swap_out = remote(columns(name, 1 - core), theirs, base, partner)
            self.swap_in = remote(ours, ours, base, partner)

            fetched, other = everything, None
            if along_z:
                fetched = pl.ds(pl.multiple_of(parity * 128, 128), 128)
                other = pl.ds(pl.multiple_of((1 - parity) * 128, 128), 128)

            def flow(name, to, out_shard, in_shard, part):
                number = base + 1 + FLOW_NAMES.index(name)
                out_part = block(out_shard, part * 256, 256, fetched)
                in_part = block(in_shard, part * 256, 256, fetched)
                return remote(out_part, out_part, number, to), remote(in_part, in_part, number, to)

            shards = {
                "below": shard(hi, down), "above": shard(hi, up), "opposite": shard(hi, across),
                "far": shard(1 - hi, y), "far_below": shard(1 - hi, down),
                "far_above": shard(1 - hi, up), "far_opposite": shard(1 - hi, across),
            }
            below, above, opposite, far, far_below, far_above, far_opposite = shards.values()
            self.flows = {
                "up_near": flow("up_near", y_next, below, opposite, 0),
                "down_near": flow("down_near", y_prev, above, opposite, 1),
            }
            for part in range(2):
                for name, to, out_shard, in_shard in (
                    ("up", y_next, mine, below),
                    ("down", y_prev, mine, above),
                    ("far", x_far, mine, far),
                    ("up_far", y_next, far, far_below),
                    ("down_far", y_prev, far, far_above),
                    ("far_across", x_far, opposite, far_opposite),
                ):
                    name += str(part)
                    self.flows[name] = flow(name, to, out_shard, in_shard, part)
            self.along = {}
            if along_z:
                for i, name in enumerate(SHARD_NAMES):
                    number = base + 1 + len(FLOW_NAMES) + i
                    to = z_next if name in along_z else z_prev
                    out_part = block(shards[name], 0, SHARD, fetched)
                    in_part = block(shards[name], 0, SHARD, other)
                    self.along[name] = (
                        remote(out_part, out_part, number, to), remote(in_part, in_part, number, to)
                    )

        def go(self, *flows):
            for f in flows:
                self.flows[f][0].start()

        def got(self, *flows):
            for f in flows:
                self.flows[f][1].wait_recv()

        def pass_on(self, *names):
            if self.along:
                for name in names:
                    self.along[name][0].start()

        def p0(self):
            self.local.wait()
            self.swap_in.wait_recv()
            self.go("up0", "down1", "far0", "far1", "up1", "down0")

        def p1(self):
            self.got("up0")
            self.go("up_near")
            self.got("down1")
            self.go("down_near")
            self.got("far0")
            self.go("up_far0", "down_far0")
            self.got("far1")
            self.go("up_far1", "down_far1")
            self.pass_on("far")

        def p2(self):
            self.got("up1")
            self.pass_on("below")
            self.got("down0")
            self.pass_on("above")
            self.got("up_near")
            self.go("far_across0")
            self.got("down_near")
            self.go("far_across1")
            self.pass_on("opposite")

        def p3(self):
            self.got("up_far0", "up_far1")
            self.pass_on("far_below")
            self.got("down_far0", "down_far1")
            self.pass_on("far_above")
            self.got("far_across0", "far_across1")
            self.pass_on("far_opposite")

        def p4(self):
            for _, landed in self.along.values():
                landed.wait_recv()

        def finish(self):
            self.swap_out.wait_send()
            for out, _ in [*self.flows.values(), *self.along.values()]:
                out.wait_send()

    k = Piece("k", along_z=("below", "above", "opposite"))
    v = Piece("v")
    qa = Piece("qa")
    qb = Piece("qb", along_z=("nothing",))
    pieces = (k, v, qa, qb)

    x_local = pltpu.make_async_copy(x_ref, xbuf.at[lo, core], local.at[4])
    for piece in pieces:
        piece.local.start()
    x_local.start()

    barrier = pltpu.get_barrier_semaphore()
    partners = (partner, y_next, y_prev, x_far, x_near, x_diag, z_next, z_prev)
    for other in partners:
        pl.semaphore_signal(barrier, inc=1, device_id=other, device_id_type=MESH)
    pl.semaphore_wait(barrier, len(partners))

    x_out = remote(x_ref, xbuf.at[lo, core], X_SWAP, partner)
    x_in = remote(xbuf.at[lo, 1 - core], xbuf.at[lo, 1 - core], X_SWAP, partner)

    def x_near_out(i):
        part = pl.ds(i * (SLAB // X_CHUNKS), SLAB // X_CHUNKS)
        return remote(x_ref.at[part], xbuf.at[lo, core, part], X_NEAR + i, x_near)

    def x_near_in(i):
        part = pl.ds(i * (SLAB // X_CHUNKS), SLAB // X_CHUNKS)
        there = xbuf.at[1 - lo, core, part]
        return remote(there, there, X_NEAR + i, x_near)

    def x_forward(piece, whose):
        there = xbuf.at[1 - lo, whose, pl.ds(piece * SLAB // 2, SLAB // 2)]
        return remote(there, there, X_FORWARD + piece, partner)

    def x_pass(piece):
        for i in range(piece * X_CHUNKS // 2, (piece + 1) * X_CHUNKS // 2):
            x_near_in(i).wait_recv()
        x_forward(piece, core).start()

    def x_got():
        for piece in range(2):
            x_forward(piece, 1 - core).wait_recv()

    for piece in pieces:
        piece.swap_out.start()
    x_out.start()

    def rope_tables():
        shape = (PAIR, HEAD_WIDTH)
        position = lax.broadcasted_iota(jnp.int32, shape, 0) + z * PAIR
        lane = lax.broadcasted_iota(jnp.int32, shape, 1)
        half = HEAD_WIDTH // 2
        exponent = (lane % half).astype(jnp.float32) * (-2.0 / HEAD_WIDTH)
        angle = position.astype(jnp.float32) * jnp.exp(exponent * LOG_ROPE_BASE)
        sine = jnp.sin(angle)
        cos_ref[...] = jnp.cos(angle).reshape(2, SLAB, HEAD_WIDTH)
        sin_ref[...] = jnp.where(lane < half, -sine, sine).reshape(2, SLAB, HEAD_WIDTH)

    def rotate(values, which):
        return values * cos_ref[which] + pltpu.roll(values, HEAD_WIDTH // 2, 1) * sin_ref[which]

    class Chain:
        def __init__(self, which, ctx, heads, buf):
            self.base = HALO + (2 * which + ctx) * PER_HALO
            self.ctx, self.heads, self.buf = ctx, heads, buf
            self.near_out = remote(
                heads.at[1 - pick, ctx], buf.at[0, ctx, lo], self.base + LEVELS, x_near
            )
            there = buf.at[0, ctx, 1 - lo]
            self.near_in = remote(there, there, self.base + LEVELS, x_near)

        def z_send(self, level):
            return remote(
                self.buf.at[level, self.ctx], self.buf.at[level + 1, self.ctx], self.base + level, z_next
            )

        def first_send(self, own):
            side = lo if own else 1 - lo
            number = self.base + (0 if own else LEVELS + 1)
            return remote(self.buf.at[0, self.ctx, side], self.buf.at[1, self.ctx, side], number, z_next)

        def open(self):
            self.buf[0, self.ctx, lo] = self.heads[pick, self.ctx]
            self.first_send(True).start()
            self.near_out.start()

        def level(self, level):
            if level == 0:
                self.near_in.wait_recv()
                self.first_send(False).start()
            elif level == 1:
                self.first_send(True).wait_recv()
                self.first_send(False).wait_recv()
            else:
                self.z_send(level - 1).wait_recv()
            if 0 < level < LEVELS:
                self.z_send(level).start()

        def finish(self):
            self.near_out.wait_send()
            self.first_send(True).wait_send()
            self.first_send(False).wait_send()
            for i in range(1, LEVELS):
                self.z_send(i).wait_send()

    k0, k1 = [Chain(0, ctx, khead, kbuf) for ctx in range(2)]
    v0, v1 = [Chain(1, ctx, vhead, vbuf) for ctx in range(2)]
    chains = (k0, k1, v0, v1)

    def project_k():
        @pl.loop(0, 2)
        def _(ctx):
            full = jnp.dot(xbuf[lo, ctx], wk[...], preferred_element_type=jnp.float32)
            for j in range(2):
                head = full[:, j * HEAD_WIDTH : (j + 1) * HEAD_WIDTH]
                khead[j, ctx] = rotate(head, lo).astype(jnp.bfloat16)

    def project_v():
        @pl.loop(0, 2)
        def _(ctx):
            full = jnp.dot(xbuf[lo, ctx], wv[...], preferred_element_type=jnp.float32)
            for j in range(2):
                vhead[j, ctx] = full[:, j * HEAD_WIDTH : (j + 1) * HEAD_WIDTH].astype(jnp.bfloat16)

    def project_q(half, w, side):
        @pl.loop(0, 2)
        def _(ctx):
            full = jnp.dot(xbuf[side, ctx], w[...], preferred_element_type=jnp.float32)
            for h in range(2):
                head = full[:, h * HEAD_WIDTH : (h + 1) * HEAD_WIDTH]
                qbuf[ctx, side, 2 * half + h] = rotate(head, side).astype(jnp.bfloat16)

    def scores(keys, ctx, side):
        queries = qbuf[ctx, side].reshape(TALL, HEAD_WIDTH)
        return lax.dot_general(
            keys, queries, (((1,), (1,)), ((), ())), preferred_element_type=jnp.float32
        )

    def weigh(values, p):
        return lax.dot_general(
            values, p.astype(jnp.bfloat16), (((0,), (0,)), ((), ())), preferred_element_type=jnp.float32
        )

    def visible(side, first_key, shape, newest):
        key = lax.broadcasted_iota(jnp.int32, shape, 0) + first_key
        token = lax.broadcasted_iota(jnp.int32, shape, 1) % SLAB + side * SLAB
        return key <= token if newest else key > token

    def begin(ctx, side):
        count = (side + 1) * SLAB
        keys = kbuf[0, ctx].reshape(PAIR, HEAD_WIDTH)[:count]
        values = vbuf[0, ctx].reshape(PAIR, HEAD_WIDTH)[:count]
        s = scores(keys, ctx, side)
        s = jnp.where(visible(side, 0, s.shape, True), s, negative_bound)
        m = jnp.max(s, axis=0, keepdims=True)
        p = jnp.exp2((s - m) * SCORE_SCALE)
        top[ctx, side] = m
        total[ctx, side] = jnp.sum(p, axis=0, keepdims=True)
        acc[ctx, side] = weigh(values, p)

    def update(ctx, side, s, values):
        old = top[ctx, side]
        m = jnp.maximum(old, jnp.max(s, axis=0, keepdims=True))
        factor = jnp.exp2((old - m) * SCORE_SCALE)
        p = jnp.exp2((s - m) * SCORE_SCALE)
        top[ctx, side] = m
        total[ctx, side] = total[ctx, side] * factor + jnp.sum(p, axis=0, keepdims=True)
        acc[ctx, side] = acc[ctx, side] * factor + weigh(values, p)

    def middle(ctx, side, level):
        keys = kbuf[level, ctx].reshape(PAIR, HEAD_WIDTH)
        values = vbuf[level, ctx].reshape(PAIR, HEAD_WIDTH)
        update(ctx, side, scores(keys, ctx, side), values)

    def oldest(ctx, side):
        first = side * SLAB
        keys = kbuf[LEVELS, ctx].reshape(PAIR, HEAD_WIDTH)[first:]
        values = vbuf[LEVELS, ctx].reshape(PAIR, HEAD_WIDTH)[first:]
        s = scores(keys, ctx, side)
        s = jnp.where(visible(side, first, s.shape, False), s, negative_bound)
        update(ctx, side, s, values)

    def attend(side, ctx, first, last):
        if first == 0:
            for static in range(2):
                pl.when(side == static)(functools.partial(begin, ctx, static))
        if last > 0:
            lax.fori_loop(
                max(first, 1), jnp.minimum(z, last) + 1,
                lambda level, c: (middle(ctx, side, level), c)[1], 0,
            )

    def conclude(ctx, side):
        for static in range(2):
            pl.when((z >= LEVELS) & (side == static))(functools.partial(oldest, ctx, static))
        result = (acc[ctx, side] / total[ctx, side]).T
        for h in range(GROUP):
            stage[side, ctx, :, h * HEAD_WIDTH : (h + 1) * HEAD_WIDTH] = result[
                h * SLAB : (h + 1) * SLAB
            ].astype(jnp.bfloat16)

    def out_columns(head):
        return out_ref.at[:, pl.ds(pl.multiple_of(head * 512, 512), 512)]

    head = 2 * core + pick

    def out_far(ctx):
        return remote(
            stage.at[1 - lo, ctx], out_columns(head), OUT + (ctx + core) % 2, device(hi, y, ctx, z, 1 - lo)
        )

    def out_partner():
        return remote(stage.at[lo, 1 - core], out_columns(head), OUT + 2, partner)

    def out_local():
        return pltpu.make_async_copy(stage.at[lo, core], out_columns(head), local.at[5])

    def close_far(ctx):
        conclude(ctx, 1 - lo)
        out_far(ctx).start()

    def close_own(ctx):
        conclude(ctx, lo)

        @pl.when(ctx == core)
        def _():
            out_local().start()

        @pl.when(ctx != core)
        def _():
            out_partner().start()

    def out_finish():
        out_local().wait()
        out_partner().wait_send()
        landed = out_columns(2 * (1 - core) + pick)
        remote(landed, landed, OUT + 2, partner).wait_recv()
        for other in range(2):
            out_far(other).wait_send()
            landed = out_columns(2 * ((core + other) % 2) + 1 - pick)
            remote(landed, landed, OUT + other, x_near).wait_recv()

    def x_go(*chunks):
        for i in chunks:
            x_near_out(i).start()

    k.p0()
    x_go(0, 1, 2)
    rope_tables()
    k.p1()
    k.p2()
    qb.p0()
    k.p3()
    qb.p1()
    x_local.wait()
    x_in.wait_recv()
    k.p4()
    project_k()
    k0.open()
    k1.open()
    x_go(3, 4)
    qb.p2()
    v.p0()
    k0.level(0)
    k1.level(0)
    qb.p3()
    v.p1()
    x_go(5)
    k0.level(1)
    k1.level(1)
    v.p2()
    qa.p0()
    k0.level(2)
    k1.level(2)
    v.p3()
    project_v()
    v0.open()
    v1.open()
    x_go(6, 7)
    qa.p1()
    k0.level(3)
    k1.level(3)
    v0.level(0)
    v1.level(0)
    qb.p4()
    project_q(1, wqb, lo)
    qa.p2()
    v0.level(1)
    k0.level(4)
    v1.level(1)
    k1.level(4)
    x_pass(0)
    qa.p3()
    project_q(0, wqa, lo)
    attend(lo, 0, 0, 1)
    v0.level(2)
    attend(lo, 1, 0, 1)
    x_pass(1)
    v1.level(2)
    attend(lo, 0, 2, 2)
    x_got()
    project_q(0, wqa, 1 - lo)
    v0.level(3)
    project_q(1, wqb, 1 - lo)
    attend(lo, 1, 2, 2)
    attend(1 - lo, 0, 0, 1)
    v1.level(3)
    attend(1 - lo, 0, 2, 3)
    attend(lo, 0, 3, 3)
    v0.level(4)
    close_far(0)
    attend(1 - lo, 1, 0, 3)
    attend(lo, 1, 3, 3)
    v1.level(4)
    close_far(1)
    close_own(0)
    close_own(1)

    for piece in pieces:
        piece.finish()
    x_out.wait_send()
    for i in range(X_CHUNKS):
        x_near_out(i).wait_send()
    for piece in range(2):
        x_forward(piece, core).wait_send()
    for chain in chains:
        chain.finish()
    out_finish()


def body(hidden_states, query_weight, key_matrix, value_matrix, context_lengths):
    x = hidden_states[0]
    seq = lax.axis_index("seq")
    any_space = pl.BlockSpec(memory_space=pl.ANY)
    bf16, f32 = jnp.bfloat16, jnp.float32
    attended = pl.pallas_call(
        kernel,
        out_shape=jax.ShapeDtypeStruct((SLAB, 2048), bf16),
        in_specs=[any_space] * 4,
        out_specs=any_space,
        scratch_shapes=[
            pltpu.VMEM((2, 2, SLAB, DEPTH), bf16),
            pltpu.VMEM((DEPTH, 256), bf16),
            pltpu.VMEM((DEPTH, 256), bf16),
            pltpu.VMEM((DEPTH, 256), bf16),
            pltpu.VMEM((DEPTH, 256), bf16),
            pltpu.VMEM((2, 2, SLAB, HEAD_WIDTH), bf16),
            pltpu.VMEM((2, 2, SLAB, HEAD_WIDTH), bf16),
            pltpu.VMEM((LEVELS + 1, 2, 2, SLAB, HEAD_WIDTH), bf16),
            pltpu.VMEM((LEVELS + 1, 2, 2, SLAB, HEAD_WIDTH), bf16),
            pltpu.VMEM((2, 2, GROUP, SLAB, HEAD_WIDTH), bf16),
            pltpu.VMEM((2, 2, SLAB, GROUP * HEAD_WIDTH), bf16),
            pltpu.VMEM((2, 2, HEAD_WIDTH, TALL), f32),
            pltpu.VMEM((2, 2, 1, TALL), f32),
            pltpu.VMEM((2, 2, 1, TALL), f32),
            pltpu.VMEM((2, SLAB, HEAD_WIDTH), f32),
            pltpu.VMEM((2, SLAB, HEAD_WIDTH), f32),
            pltpu.SemaphoreType.DMA((FLOWS,)),
            pltpu.SemaphoreType.DMA((FLOWS,)),
            pltpu.SemaphoreType.DMA((6,)),
        ],
        compiler_params=pltpu.CompilerParams(
            collective_id=0, has_side_effects=True, vmem_limit_bytes=56 * 2**20
        ),
        name="gather_project_attend",
    )(x, query_weight, key_matrix, value_matrix)
    positions = seq * SLAB + jnp.arange(SLAB, dtype=jnp.int32)
    valid = positions < context_lengths[0]
    return jnp.where(valid[:, None], attended, jnp.zeros_like(attended))[None]


def solution(mesh):
    return jax.shard_map(
        body,
        mesh=mesh,
        in_specs=(P("dp", "seq", None), P("dp", None), P("dp", None), P("dp", None), P("dp")),
        out_specs=P("dp", "seq", None),
        check_vma=False,
    )
```

time: 109 us -> 102 us (0.936); the launches traced: 109 us -> 100 us
  Pallas kernels: 104 us -> 97.3 us
  other arithmetic: 4.37 us -> 2.34 us
    pallas_call x1, Pallas kernels: 104 us -> 97.3 us  [body(): pl.pallas_call(kernel, out_shape=jax.ShapeDtypeStruct((SLAB, 2048), bf16)...]
where the time goes in v3:
time: 102 us; the launch traced here: 100 us
  Pallas kernels  97.3 us (95%)
  other arithmetic  2.34 us (2%)
    pallas_call x1, Pallas kernels, body(): pl.pallas_call(kernel, out_shape=jax.ShapeDtypeStruct((SLAB, 2048), bf16)...  97.3 us
    broadcast_in_dim x1, other arithmetic, body(): return jnp.where(valid[:, None], attended, jnp.zeros_like(attended))[None]  2.34 us

profile of v3, /device:TPU:161, one launch (start us, length us, event | category | flops | bytes accessed | tf_op | source)
XLA Modules:
  0.0 100.3 jit_solution(12905520053886838309)
XLA Ops:
  0.7 97.3 %gather_project_attend.1 = bf16[256,2048]{1,0:T(8,128)(2,1)} custom-call(bf16[256,4096]{1,0:T(8,128)(2,1)} %bitcast.5, bf16[256,2048]{1,0:T(8,128)(2,1)} %wq_ref.1, bf16[256,512]{1,0:T(8,128)(2,1)} %wk_ref.1, bf16[256,512]{1,0:T(8,128)(2,1)} %wv_ref.1), custom_call_target="tpu_custom_call" | custom-call | tf_op jit(solution)/shard_map/gather_project_attend/pallas_call | solution.py:536
  98.0 2.3 %select_bitcast_fusion = bf16[1,256,2048]{2,1,0:T(8,128)(2,1)} fusion(bf16[256,2048]{1,0:T(8,128)(2,1)} %gather_project_attend.1, pred[256]{0:T(512)(128)(4,1)S(1)} %add_compare_fusion), kind=kLoop, calls=%fused_computation | loop fusion | flops 524288 | bytes 2097408 | tf_op jit(solution)/shard_map/broadcast_in_dim | solution.py:569
  (1 shorter events, 0.0 us)

commit v4 on v3

--- a/solution.py
+++ b/solution.py
@@ -36,12 +36,13 @@
 X_SWAP = OUT + PER_OUT
 X_NEAR = X_SWAP + 1
 X_FORWARD = X_NEAR + X_CHUNKS
-FLOWS = X_FORWARD + 2
+BACK = X_FORWARD + 2
+FLOWS = BACK + 4 * LEVELS
 
 
 def kernel(
     x_ref, wq_ref, wk_ref, wv_ref, out_ref,
-    xbuf, wk, wv, wqa, wqb, khead, vhead, kbuf, vbuf, qbuf, stage, acc, top, total, cos_ref, sin_ref,
+    xbuf, wk, wv, wqa, wqb, khead, vhead, kbuf, vbuf, kback, vback, qbuf, stage, acc, top, total, cos_ref, sin_ref,
     send, recv, local,
 ):
     dp, seq = lax.axis_index("dp"), lax.axis_index("seq")
@@ -260,8 +261,9 @@
         return values * cos_ref[which] + pltpu.roll(values, HEAD_WIDTH // 2, 1) * sin_ref[which]
 
     class Chain:
-        def __init__(self, which, ctx, heads, buf):
-            self.base = HALO + (2 * which + ctx) * PER_HALO
+        def __init__(self, which, turn, heads, buf):
+            self.base = HALO + (2 * which + turn) * PER_HALO
+            ctx = order[turn]
             self.ctx, self.heads, self.buf = ctx, heads, buf
             self.near_out = remote(
                 heads.at[1 - pick, ctx], buf.at[0, ctx, lo], self.base + LEVELS, x_near
@@ -270,19 +272,24 @@
             self.near_in = remote(there, there, self.base + LEVELS, x_near)
 
         def z_send(self, level):
-            return remote(
-                self.buf.at[level, self.ctx], self.buf.at[level + 1, self.ctx], self.base + level, z_next
-            )
+            src, dst = self.buf.at[level, self.ctx], self.buf.at[level + 1, self.ctx]
+            if level == LEVELS - 1:
+                src, dst = src.at[1], dst.at[1]
+            return remote(src, dst, self.base + level, z_next)
 
         def first_send(self, own):
             side = lo if own else 1 - lo
             number = self.base + (0 if own else LEVELS + 1)
             return remote(self.buf.at[0, self.ctx, side], self.buf.at[1, self.ctx, side], number, z_next)
 
-        def open(self):
+        def near(self):
+            self.near_out.start()
+
+        def open(self, near=False):
             self.buf[0, self.ctx, lo] = self.heads[pick, self.ctx]
             self.first_send(True).start()
-            self.near_out.start()
+            if near:
+                self.near()
 
         def level(self, level):
             if level == 0:
@@ -303,8 +310,31 @@
             for i in range(1, LEVELS):
                 self.z_send(i).wait_send()
 
-    k0, k1 = [Chain(0, ctx, khead, kbuf) for ctx in range(2)]
-    v0, v1 = [Chain(1, ctx, vhead, vbuf) for ctx in range(2)]
+    class Back:
+        def __init__(self, which, turn, buf, slots):
+            self.base = BACK + (2 * which + turn) * LEVELS
+            ctx = order[turn]
+            between = [slots.at[i, ctx] for i in range(LEVELS - 1)]
+            self.places = [buf.at[0, ctx, 0], *between, buf.at[LEVELS, ctx, 0]]
+
+        def send(self, hop):
+            return remote(self.places[hop], self.places[hop + 1], self.base + hop, z_prev)
+
+        def hop(self, hop):
+            if hop > 0:
+                self.send(hop - 1).wait_recv()
+            if hop < LEVELS:
+                self.send(hop).start()
+
+        def finish(self):
+            for hop in range(LEVELS):
+                self.send(hop).wait_send()
+
+    order = (core, 1 - core)
+    kb0, kb1 = [Back(0, turn, kbuf, kback) for turn in range(2)]
+    vb0, vb1 = [Back(1, turn, vbuf, vback) for turn in range(2)]
+    k0, k1 = [Chain(0, turn, khead, kbuf) for turn in range(2)]
+    v0, v1 = [Chain(1, turn, vhead, vbuf) for turn in range(2)]
     chains = (k0, k1, v0, v1)
 
     def project_k():
@@ -322,13 +352,15 @@
             for j in range(2):
                 vhead[j, ctx] = full[:, j * HEAD_WIDTH : (j + 1) * HEAD_WIDTH].astype(jnp.bfloat16)
 
-    def project_q(half, w, side):
-        @pl.loop(0, 2)
-        def _(ctx):
-            full = jnp.dot(xbuf[side, ctx], w[...], preferred_element_type=jnp.float32)
-            for h in range(2):
-                head = full[:, h * HEAD_WIDTH : (h + 1) * HEAD_WIDTH]
-                qbuf[ctx, side, 2 * half + h] = rotate(head, side).astype(jnp.bfloat16)
+    def project_q(half, w, side, ctx):
+        full = jnp.dot(xbuf[side, ctx], w[...], preferred_element_type=jnp.float32)
+        for h in range(2):
+            head = full[:, h * HEAD_WIDTH : (h + 1) * HEAD_WIDTH]
+            qbuf[ctx, side, 2 * half + h] = rotate(head, side).astype(jnp.bfloat16)
+
+    def project_side(side, ctx):
+        project_q(0, wqa, side, ctx)
+        project_q(1, wqb, side, ctx)
 
     def scores(keys, ctx, side):
         queries = qbuf[ctx, side].reshape(TALL, HEAD_WIDTH)
@@ -404,10 +436,9 @@
 
     head = 2 * core + pick
 
-    def out_far(ctx):
-        return remote(
-            stage.at[1 - lo, ctx], out_columns(head), OUT + (ctx + core) % 2, device(hi, y, ctx, z, 1 - lo)
-        )
+    def out_far(turn):
+        to = (x_near, x_diag)[turn]
+        return remote(stage.at[1 - lo, order[turn]], out_columns(head), OUT + turn, to)
 
     def out_partner():
         return remote(stage.at[lo, 1 - core], out_columns(head), OUT + 2, partner)
@@ -415,19 +446,15 @@
     def out_local():
         return pltpu.make_async_copy(stage.at[lo, core], out_columns(head), local.at[5])
 
-    def close_far(ctx):
-        conclude(ctx, 1 - lo)
-        out_far(ctx).start()
-
-    def close_own(ctx):
-        conclude(ctx, lo)
-
-        @pl.when(ctx == core)
-        def _():
+    def close_far(turn):
+        conclude(order[turn], 1 - lo)
+        out_far(turn).start()
+
+    def close_own(turn):
+        conclude(order[turn], lo)
+        if turn == 0:
             out_local().start()
-
-        @pl.when(ctx != core)
-        def _():
+        else:
             out_partner().start()
 
     def out_finish():
@@ -435,10 +462,13 @@
         out_partner().wait_send()
         landed = out_columns(2 * (1 - core) + pick)
         remote(landed, landed, OUT + 2, partner).wait_recv()
-        for other in range(2):
-            out_far(other).wait_send()
-            landed = out_columns(2 * ((core + other) % 2) + 1 - pick)
-            remote(landed, landed, OUT + other, x_near).wait_recv()
+        for turn in range(2):
+            out_far(turn).wait_send()
+            landed = out_columns(2 * order[turn] + 1 - pick)
+            remote(landed, landed, OUT + turn, x_near).wait_recv()
+
+    first, second = order
+    far = 1 - lo
 
     def x_go(*chunks):
         for i in chunks:
@@ -456,13 +486,15 @@
     x_in.wait_recv()
     k.p4()
     project_k()
-    k0.open()
-    k1.open()
+    k0.open(True)
+    k1.open(True)
     x_go(3, 4)
     qb.p2()
     v.p0()
     k0.level(0)
     k1.level(0)
+    kb0.hop(0)
+    kb1.hop(0)
     qb.p3()
     v.p1()
     x_go(5)
@@ -472,48 +504,66 @@
     qa.p0()
     k0.level(2)
     k1.level(2)
+    kb0.hop(1)
+    kb1.hop(1)
     v.p3()
     project_v()
-    v0.open()
-    v1.open()
+    v0.open(True)
+    v1.near()
     x_go(6, 7)
-    qa.p1()
     k0.level(3)
     k1.level(3)
+    qa.p1()
     v0.level(0)
+    vb0.hop(0)
+    kb0.hop(2)
+    kb1.hop(2)
+    qb.p4()
+    project_q(1, wqb, lo, first)
+    project_q(1, wqb, lo, second)
+    v0.level(1)
+    v1.open()
     v1.level(0)
-    qb.p4()
-    project_q(1, wqb, lo)
+    vb0.hop(1)
+    vb1.hop(0)
     qa.p2()
-    v0.level(1)
     k0.level(4)
-    v1.level(1)
     k1.level(4)
+    kb0.hop(3)
+    kb1.hop(3)
     x_pass(0)
     qa.p3()
-    project_q(0, wqa, lo)
-    attend(lo, 0, 0, 1)
+    project_q(0, wqa, lo, first)
     v0.level(2)
-    attend(lo, 1, 0, 1)
+    vb0.hop(2)
+    project_q(0, wqa, lo, second)
+    v1.level(1)
+    vb1.hop(1)
+    attend(lo, first, 0, 1)
     x_pass(1)
+    project_side(far, first)
+    v0.level(3)
+    attend(lo, first, 2, 2)
+    vb0.hop(3)
     v1.level(2)
-    attend(lo, 0, 2, 2)
-    x_got()
-    project_q(0, wqa, 1 - lo)
-    v0.level(3)
-    project_q(1, wqb, 1 - lo)
-    attend(lo, 1, 2, 2)
-    attend(1 - lo, 0, 0, 1)
-    v1.level(3)
-    attend(1 - lo, 0, 2, 3)
-    attend(lo, 0, 3, 3)
+    vb1.hop(2)
+    attend(far, first, 0, 3)
+    kb0.hop(4)
+    kb1.hop(4)
+    vb0.hop(4)
     v0.level(4)
     close_far(0)
-    attend(1 - lo, 1, 0, 3)
-    attend(lo, 1, 3, 3)
+    v1.level(3)
+    vb1.hop(3)
+    x_got()
+    project_side(far, second)
+    attend(far, second, 0, 3)
+    attend(lo, first, 3, 3)
+    close_own(0)
+    vb1.hop(4)
     v1.level(4)
     close_far(1)
-    close_own(0)
+    attend(lo, second, 0, 3)
     close_own(1)
 
     for piece in pieces:
@@ -523,7 +573,7 @@
         x_near_out(i).wait_send()
     for piece in range(2):
         x_forward(piece, core).wait_send()
-    for chain in chains:
+    for chain in (*chains, kb0, kb1, vb0, vb1):
         chain.finish()
     out_finish()
 
@@ -548,6 +598,8 @@
             pltpu.VMEM((2, 2, SLAB, HEAD_WIDTH), bf16),
             pltpu.VMEM((LEVELS + 1, 2, 2, SLAB, HEAD_WIDTH), bf16),
             pltpu.VMEM((LEVELS + 1, 2, 2, SLAB, HEAD_WIDTH), bf16),
+            pltpu.VMEM((LEVELS - 1, 2, SLAB, HEAD_WIDTH), bf16),
+            pltpu.VMEM((LEVELS - 1, 2, SLAB, HEAD_WIDTH), bf16),
             pltpu.VMEM((2, 2, GROUP, SLAB, HEAD_WIDTH), bf16),
             pltpu.VMEM((2, 2, SLAB, GROUP * HEAD_WIDTH), bf16),
             pltpu.VMEM((2, 2, HEAD_WIDTH, TALL), f32),

time: 102 us -> 99.4 us (0.975); the launches traced: 100 us -> 99.3 us
  no operation moved by 1% of the time
where the time goes in v4:
time: 99.4 us; the launch traced here: 99.3 us
  Pallas kernels  96.3 us (97%)
  other arithmetic  2.34 us (2%)
    pallas_call x1, Pallas kernels, body(): pl.pallas_call(kernel, out_shape=jax.ShapeDtypeStruct((SLAB, 2048), bf16)...  96.3 us
    broadcast_in_dim x1, other arithmetic, body(): return jnp.where(valid[:, None], attended, jnp.zeros_like(attended))[None]  2.34 us

profile of v4, /device:TPU:161, one launch (start us, length us, event | category | flops | bytes accessed | tf_op | source)
XLA Modules:
  0.0 99.3 jit_solution(743353759210928872)
XLA Ops:
  0.7 96.3 %gather_project_attend.1 = bf16[256,2048]{1,0:T(8,128)(2,1)} custom-call(bf16[256,4096]{1,0:T(8,128)(2,1)} %bitcast.5, bf16[256,2048]{1,0:T(8,128)(2,1)} %wq_ref.1, bf16[256,512]{1,0:T(8,128)(2,1)} %wk_ref.1, bf16[256,512]{1,0:T(8,128)(2,1)} %wv_ref.1), custom_call_target="tpu_custom_call" | custom-call | tf_op jit(solution)/shard_map/gather_project_attend/pallas_call | solution.py:586
  97.0 2.3 %select_bitcast_fusion = bf16[1,256,2048]{2,1,0:T(8,128)(2,1)} fusion(bf16[256,2048]{1,0:T(8,128)(2,1)} %gather_project_attend.1, pred[256]{0:T(512)(128)(4,1)S(1)} %add_compare_fusion), kind=kLoop, calls=%fused_computation | loop fusion | flops 524288 | bytes 2097408 | tf_op jit(solution)/shard_map/broadcast_in_dim | solution.py:621
  (1 shorter events, 0.0 us)

commit v5 on v4

--- a/solution.py
+++ b/solution.py
@@ -200,7 +200,7 @@
             for out, _ in [*self.flows.values(), *self.along.values()]:
                 out.wait_send()
 
-    k = Piece("k", along_z=("below", "above", "opposite"))
+    k = Piece("k", along_z=("below", "above", "far_above", "far_opposite"))
     v = Piece("v")
     qa = Piece("qa")
     qb = Piece("qb", along_z=("nothing",))
@@ -509,24 +509,25 @@
     v.p3()
     project_v()
     v0.open(True)
-    v1.near()
+    v1.open(True)
     x_go(6, 7)
     k0.level(3)
     k1.level(3)
     qa.p1()
     v0.level(0)
+    v1.level(0)
     vb0.hop(0)
+    vb1.hop(0)
     kb0.hop(2)
     kb1.hop(2)
     qb.p4()
     project_q(1, wqb, lo, first)
     project_q(1, wqb, lo, second)
+    qa.p2()
     v0.level(1)
-    v1.open()
-    v1.level(0)
+    v1.level(1)
     vb0.hop(1)
-    vb1.hop(0)
-    qa.p2()
+    vb1.hop(1)
     k0.level(4)
     k1.level(4)
     kb0.hop(3)
@@ -534,36 +535,36 @@
     x_pass(0)
     qa.p3()
     project_q(0, wqa, lo, first)
+    project_q(0, wqa, lo, second)
+    attend(lo, first, 0, 1)
     v0.level(2)
     vb0.hop(2)
-    project_q(0, wqa, lo, second)
-    v1.level(1)
-    vb1.hop(1)
-    attend(lo, first, 0, 1)
+    attend(lo, second, 0, 1)
+    v1.level(2)
+    vb1.hop(2)
     x_pass(1)
     project_side(far, first)
+    attend(far, first, 0, 1)
     v0.level(3)
-    attend(lo, first, 2, 2)
     vb0.hop(3)
-    v1.level(2)
-    vb1.hop(2)
-    attend(far, first, 0, 3)
+    attend(far, first, 2, 2)
+    v1.level(3)
+    vb1.hop(3)
+    attend(far, first, 3, 3)
     kb0.hop(4)
     kb1.hop(4)
     vb0.hop(4)
     v0.level(4)
     close_far(0)
-    v1.level(3)
-    vb1.hop(3)
     x_got()
     project_side(far, second)
     attend(far, second, 0, 3)
-    attend(lo, first, 3, 3)
-    close_own(0)
     vb1.hop(4)
     v1.level(4)
     close_far(1)
-    attend(lo, second, 0, 3)
+    attend(lo, first, 2, 3)
+    close_own(0)
+    attend(lo, second, 2, 3)
     close_own(1)
 
     for piece in pieces:

time: 99.4 us -> 96.1 us (0.967)
  Pallas kernels: 96.3 us -> 92.6 us
    pallas_call x1, Pallas kernels: 96.3 us -> 92.6 us  [body(): pl.pallas_call(kernel, out_shape=jax.ShapeDtypeStruct((SLAB, 2048), bf16)...]
where the time goes in v5:
time: 96.1 us; the launch traced here: 95.6 us
  Pallas kernels  92.6 us (96%)
  other arithmetic  2.34 us (2%)
    pallas_call x1, Pallas kernels, body(): pl.pallas_call(kernel, out_shape=jax.ShapeDtypeStruct((SLAB, 2048), bf16)...  92.6 us
    broadcast_in_dim x1, other arithmetic, body(): return jnp.where(valid[:, None], attended, jnp.zeros_like(attended))[None]  2.34 us

profile of v5, /device:TPU:161, one launch (start us, length us, event | category | flops | bytes accessed | tf_op | source)
XLA Modules:
  0.0 95.6 jit_solution(3673251283740062658)
XLA Ops:
  0.7 92.6 %gather_project_attend.1 = bf16[256,2048]{1,0:T(8,128)(2,1)} custom-call(bf16[256,4096]{1,0:T(8,128)(2,1)} %bitcast.5, bf16[256,2048]{1,0:T(8,128)(2,1)} %wq_ref.1, bf16[256,512]{1,0:T(8,128)(2,1)} %wk_ref.1, bf16[256,512]{1,0:T(8,128)(2,1)} %wv_ref.1), custom_call_target="tpu_custom_call" | custom-call | tf_op jit(solution)/shard_map/gather_project_attend/pallas_call | solution.py:587
  93.3 2.3 %select_bitcast_fusion = bf16[1,256,2048]{2,1,0:T(8,128)(2,1)} fusion(bf16[256,2048]{1,0:T(8,128)(2,1)} %gather_project_attend.1, pred[256]{0:T(512)(128)(4,1)S(1)} %add_compare_fusion), kind=kLoop, calls=%fused_computation | loop fusion | flops 524288 | bytes 2097408 | tf_op jit(solution)/shard_map/broadcast_in_dim | solution.py:622
  (1 shorter events, 0.0 us)

commit v6 on v5

--- a/solution.py
+++ b/solution.py
@@ -399,9 +399,9 @@
         total[ctx, side] = total[ctx, side] * factor + jnp.sum(p, axis=0, keepdims=True)
         acc[ctx, side] = acc[ctx, side] * factor + weigh(values, p)
 
-    def middle(ctx, side, level):
-        keys = kbuf[level, ctx].reshape(PAIR, HEAD_WIDTH)
-        values = vbuf[level, ctx].reshape(PAIR, HEAD_WIDTH)
+    def middle(ctx, side, level, count=1):
+        keys = kbuf[pl.ds(level, count), ctx].reshape(count * PAIR, HEAD_WIDTH)
+        values = vbuf[pl.ds(level, count), ctx].reshape(count * PAIR, HEAD_WIDTH)
         update(ctx, side, scores(keys, ctx, side), values)
 
     def oldest(ctx, side):
@@ -416,11 +416,21 @@
         if first == 0:
             for static in range(2):
                 pl.when(side == static)(functools.partial(begin, ctx, static))
-        if last > 0:
-            lax.fori_loop(
-                max(first, 1), jnp.minimum(z, last) + 1,
-                lambda level, c: (middle(ctx, side, level), c)[1], 0,
-            )
+        start = max(first, 1)
+        if last > start:
+
+            @pl.when(z >= last)
+            def _():
+                middle(ctx, side, start, last - start + 1)
+
+        if last >= start:
+
+            @pl.when((z < last) | (last == start))
+            def _():
+                lax.fori_loop(
+                    start, jnp.minimum(z, last) + 1,
+                    lambda level, c: (middle(ctx, side, level), c)[1], 0,
+                )
 
     def conclude(ctx, side):
         for static in range(2):
@@ -535,19 +545,18 @@
     x_pass(0)
     qa.p3()
     project_q(0, wqa, lo, first)
+    v0.level(2)
     project_q(0, wqa, lo, second)
+    vb0.hop(2)
     attend(lo, first, 0, 1)
-    v0.level(2)
-    vb0.hop(2)
-    attend(lo, second, 0, 1)
     v1.level(2)
     vb1.hop(2)
+    attend(lo, second, 0, 0)
     x_pass(1)
     project_side(far, first)
-    attend(far, first, 0, 1)
     v0.level(3)
     vb0.hop(3)
-    attend(far, first, 2, 2)
+    attend(far, first, 0, 2)
     v1.level(3)
     vb1.hop(3)
     attend(far, first, 3, 3)
@@ -564,7 +573,7 @@
     close_far(1)
     attend(lo, first, 2, 3)
     close_own(0)
-    attend(lo, second, 2, 3)
+    attend(lo, second, 1, 3)
     close_own(1)
 
     for piece in pieces:

time: 96.1 us -> 93.9 us (0.977)
  Pallas kernels: 92.6 us -> 90.2 us
    pallas_call x1, Pallas kernels: 92.6 us -> 90.2 us  [body(): pl.pallas_call(kernel, out_shape=jax.ShapeDtypeStruct((SLAB, 2048), bf16)...]
where the time goes in v6:
time: 93.9 us; the launch traced here: 93.3 us
  Pallas kernels  90.2 us (96%)
  other arithmetic  2.34 us (2%)
    pallas_call x1, Pallas kernels, body(): pl.pallas_call(kernel, out_shape=jax.ShapeDtypeStruct((SLAB, 2048), bf16)...  90.2 us
    broadcast_in_dim x1, other arithmetic, body(): return jnp.where(valid[:, None], attended, jnp.zeros_like(attended))[None]  2.34 us

profile of v6, /device:TPU:161, one launch (start us, length us, event | category | flops | bytes accessed | tf_op | source)
XLA Modules:
  0.0 93.3 jit_solution(14993469095994858895)
XLA Ops:
  0.7 90.2 %gather_project_attend.1 = bf16[256,2048]{1,0:T(8,128)(2,1)} custom-call(bf16[256,4096]{1,0:T(8,128)(2,1)} %bitcast.5, bf16[256,2048]{1,0:T(8,128)(2,1)} %wq_ref.1, bf16[256,512]{1,0:T(8,128)(2,1)} %wk_ref.1, bf16[256,512]{1,0:T(8,128)(2,1)} %wv_ref.1), custom_call_target="tpu_custom_call" | custom-call | tf_op jit(solution)/shard_map/gather_project_attend/pallas_call | solution.py:596
  90.9 2.3 %select_bitcast_fusion = bf16[1,256,2048]{2,1,0:T(8,128)(2,1)} fusion(bf16[256,2048]{1,0:T(8,128)(2,1)} %gather_project_attend.1, pred[256]{0:T(512)(128)(4,1)S(1)} %add_compare_fusion), kind=kLoop, calls=%fused_computation | loop fusion | flops 524288 | bytes 2097408 | tf_op jit(solution)/shard_map/broadcast_in_dim | solution.py:631
  (1 shorter events, 0.0 us)
